TPU v7x, 32 devices: a whole 2x2x4 slice. The times are simulated.
32 devices in a mesh: bins: 8 (over y, x, core), batch: 4 (over z).
Axes of the slice: x: 2, y: 2, z: 4, core: 2. Of those that a mesh axis runs over, the one named last changes fastest.
Arguments:
- block_in: bfloat16 [16, 2048, 768], P('batch', 'bins')
- gain_in: float32 [768], replicated, may hold values from 0.5 to 1.5
- shift_in: float32 [768], replicated, may hold values from -2 to 2
- dilated_taps_weight: bfloat16 [3, 768, 384], replicated, may hold values from -0.125 to 0.125
- gain_mid: float32 [384], replicated, may hold values from 0.5 to 1.5
- shift_mid: float32 [384], replicated, may hold values from -2 to 2
- proj_weight: bfloat16 [384, 768], replicated, may hold values from -0.3125 to 0.3125
- proj_bias: float32 [768], replicated, may hold values from -2 to 2
- head_human: bfloat16 [768, 5313], replicated, may hold values from -0.21875 to 0.21875
- bias_human: float32 [5313], replicated, may hold values from -3 to 3
- head_mouse: bfloat16 [768, 1643], replicated, may hold values from -0.21875 to 0.21875
- bias_mouse: float32 [1643], replicated, may hold values from -3 to 3
- species: int32 [16], P('batch'), may hold values 0 or 1
- counts: int32 [16, 2048, 5313], P('batch', 'bins'), may hold values from 0 to 5
Outputs:
- block_out: bfloat16 [16, 2048, 768], P('batch', 'bins')
- input_grad: bfloat16 [16, 2048, 768], P('batch', 'bins')
- gain_in_grad: float32 [768], replicated
- shift_in_grad: float32 [768], replicated
- conv_grad: float32 [3, 768, 384], replicated
- gain_mid_grad: float32 [384], replicated
- shift_mid_grad: float32 [384], replicated
- proj_grad: float32 [384, 768], replicated
- proj_bias_grad: float32 [768], replicated
- head_human_grad: float32 [768, 5313], replicated
- bias_human_grad: float32 [5313], replicated
- head_mouse_grad: float32 [768, 1643], replicated
- bias_mouse_grad: float32 [1643], replicated
Inputs may be any that keep to these rules, and one draw needn't show every extreme that they name: `species`: 0 marks a human window, 1 a mouse window.
All inputs are finite; a program needn't handle non-finite values. No bound on the sum of `species` on one device may be relied on, other than what follows from the above.
Results may differ from a plain program's by a relative error of at most 0.0063.
Values may be sent and summed in bfloat16 or wider, within the bound.
No kernel may reach another device: no remote copies, remote signals or barrier semaphores. Data moves between devices by JAX's collectives and lax.ppermute only.
A program may use at most 192 MiB of HBM per device.

v0:
```python
import functools
import math

import jax
import jax.numpy as jnp
from jax import lax
from jax.experimental import pallas as pl
from jax.experimental.pallas import tpu as pltpu
from jax.sharding import PartitionSpec as P

DILATION_STEP = 11
EPS = 1e-05
F32 = jnp.float32
BF16 = jnp.bfloat16
EVERY = ("y", "x", "core", "batch")
BINS = ("y", "x", "core")
CHIPS = ("y", "x", "batch")
CORE = ("core", 1)
LANES = 128
TILE = 896


def bits_of(axis):
    return [(axis, 1 << i) for i in range(lax.axis_size(axis).bit_length() - 1)]


def small_sum(parts):
    flat = jnp.concatenate([part.reshape(-1) for part in parts])
    peers = lax.axis_size(EVERY)
    sent = jnp.broadcast_to(flat[None], (peers, flat.shape[0]))
    cuts = [part.size for part in parts]

    def finish(everyone):
        total = jnp.sum(everyone, axis=0)
        ends = [sum(cuts[: i + 1]) for i in range(len(cuts))]
        return [
            total[end - cut : end].reshape(part.shape)
            for part, cut, end in zip(parts, cuts, ends)
        ]

    return sent, finish


def to_all(sent, axes=EVERY):
    return lax.all_to_all(sent, axes, 0, 0, tiled=True)


def swap(value, stage):
    axis, mask = stage
    size = lax.axis_size(axis)
    return lax.ppermute(value, axis, [(i, i ^ mask) for i in range(size)])


def upper(stage):
    axis, mask = stage
    return ((lax.axis_index(axis) & mask) != 0).astype(jnp.int32)


class Stream:
    def __init__(self, pieces, stages):
        self.held = [(piece, 0) for piece in pieces]
        self.rows = pieces[0].shape[0]
        self.up = list(stages)
        self.down = list(reversed(stages))
        self.share = None

    def busy(self):
        return bool(self.up or self.down)

    def part(self, which):
        return sum(
            lax.dynamic_slice_in_dim(piece, at + which * self.rows, self.rows, 0).astype(F32)
            for piece, at in self.held
        ).astype(BF16)

    def outgoing(self):
        if self.up:
            self.rows //= 2
            return self.part(1 - upper(self.up[0]))
        if self.share is None:
            self.share = self.part(0)
        return self.share

    def exchange(self, value):
        return swap(value, self.up[0] if self.up else self.down[0])

    def incoming(self, arrived):
        if self.up:
            mine = upper(self.up.pop(0))
            self.held = [(piece, at + mine * self.rows) for piece, at in self.held]
            self.held.append((arrived, 0))
            return
        mine = upper(self.down.pop(0))
        self.share = jnp.concatenate(
            [
                jnp.where(mine == 1, arrived, self.share),
                jnp.where(mine == 1, self.share, arrived),
            ],
            axis=0,
        )


def together(transfers, work, given):
    values, given = lax.optimization_barrier(([value for value, _ in transfers], given))
    arrived = [move(value) for value, (_, move) in zip(values, transfers)]
    return lax.optimization_barrier((arrived, work(*given)))


def advance(streams, more=(), work=lambda: (), given=()):
    streams = [stream for stream in streams if stream.busy()]
    transfers = [(stream.outgoing(), stream.exchange) for stream in streams] + list(more)
    arrived, result = together(transfers, work, given)
    for stream, value in zip(streams, arrived):
        stream.incoming(value)
    return arrived[len(streams) :], result


def gelu_pair(values):
    logistic = jax.nn.sigmoid(1.702 * values)
    return (values * logistic, logistic + 1.702 * values * logistic * (1.0 - logistic))


def rows_product(former, latter):
    return lax.dot_general(
        former, latter, (((0,), (0,)), ((), ())), preferred_element_type=F32
    )


def back_product(former, latter):
    return lax.dot_general(
        former, latter, (((1,), (1,)), ((), ())), preferred_element_type=F32
    )


def taps(padded_rows, span):
    windows = padded_rows.shape[0]
    return [
        padded_rows[:, k * DILATION_STEP : k * DILATION_STEP + span, :].reshape(
            windows * span, -1
        )
        for k in range(3)
    ]


def statistics(plain_sum, square_sum, population):
    centre = plain_sum / population
    return (centre, lax.rsqrt(square_sum / population - centre * centre + EPS))


def edges(shard, width):
    peers, length = (lax.axis_size(BINS), shard.shape[1])
    up = [(i, i + 1) for i in range(peers - 1)]
    down = [(i + 1, i) for i in range(peers - 1)]
    return (
        (shard[:, length - width :], lambda value: lax.ppermute(value, BINS, up)),
        (shard[:, :width], lambda value: lax.ppermute(value, BINS, down)),
    )


def poisson_slope(logits, counted):
    small = jnp.exp(-jnp.abs(logits))
    whole = 1.0 + small
    inverse = 1.0 / whole
    logistic = jnp.where(logits >= 0.0, inverse, small * inverse)
    tail = jnp.where(small < 1e-3, small * (1.0 - 0.5 * small), jnp.log(whole))
    ratio = logistic / (jnp.maximum(logits, 0.0) + tail)
    return logistic - counted * jnp.where(logits < -20.0, 1.0, ratio)


def head_body(
    species_ref,
    core_ref,
    weight_ref,
    bias_ref,
    counts_ref,
    rows_ref,
    columns_ref,
    before_ref,
    keep_ref,
    send_ref,
    after_ref,
    bias_grad_ref,
    grads_ref,
    bias_wide_ref,
    bias_sum_ref,
    *,
    tracks,
    first,
    which,
    scale,
):
    step = pl.program_id(0)
    tile, width = weight_ref.shape
    windows = species_ref.shape[0]
    span = rows_ref.shape[0] // windows
    lane = min(span, LANES)
    groups = span // lane
    track = (first + step) * tile + lax.broadcasted_iota(jnp.int32, (tile, 1), 0)
    inside = track < tracks

    @pl.when(step == 0)
    def _():
        after_ref[...] = before_ref[...]

    active = sum((species_ref[i] == which).astype(jnp.int32) for i in range(windows))
    weight = jnp.where(inside, weight_ref[...], BF16(0))
    weight_t = weight.T
    bias_wide_ref[...] = jnp.broadcast_to(bias_ref[...], (LANES, tile)).T
    bias_sum_ref[...] = jnp.zeros_like(bias_sum_ref)

    def window(i):
        lanes = slice(i * span, (i + 1) * span)
        logits = jnp.dot(weight, columns_ref[:, lanes], preferred_element_type=F32)
        total = jnp.zeros((tile, lane), F32)
        low = []
        for h in range(groups):
            counted = counts_ref[
                pl.ds(h * windows + i, tile, stride=groups * windows), :
            ].astype(F32)
            part = logits[:, h * lane : (h + 1) * lane] + bias_wide_ref[:, :lane]
            slope = jnp.where(inside, poisson_slope(part, counted) * scale, 0.0)
            total = total + slope
            low.append(slope.astype(BF16))
        low = jnp.concatenate(low, axis=1)
        grads_ref[:, lanes] = low
        after_ref[:, lanes] += jnp.dot(weight_t, low, preferred_element_type=F32)
        bias_sum_ref[...] += total

    @pl.when(active == windows)
    def _():
        for i in range(windows):
            window(i)

    @pl.when(active < windows)
    def _():
        for i in range(windows):

            @pl.when(species_ref[i] == which)
            def _():
                window(i)

            @pl.when(species_ref[i] != which)
            def _():
                grads_ref[:, i * span : (i + 1) * span] = jnp.zeros((tile, span), BF16)

    bias_grad_ref[...] = jnp.sum(bias_sum_ref[...].T, axis=0, keepdims=True)

    def store(left, right):
        @pl.when(core_ref[0] == 0)
        def _():
            keep_ref[...] = left
            send_ref[...] = right

        @pl.when(core_ref[0] != 0)
        def _():
            keep_ref[...] = right
            send_ref[...] = left

    @pl.when(active > 0)
    def _():
        product = jnp.dot(grads_ref[...], rows_ref[...], preferred_element_type=F32).astype(BF16)
        store(product[:, : width // 2], product[:, width // 2 :])

    @pl.when(active == 0)
    def _():
        nothing = jnp.zeros((tile, width // 2), BF16)
        store(nothing, nothing)


def head(species, core, weight, bias, counts, rows, columns, before, first, tiles, which, scale):
    tracks, width = weight.shape
    tokens = rows.shape[0]
    every = tokens // counts.shape[1]
    at = lambda j, *_: (first + j, 0)
    across = lambda j, *_: (0, first + j)
    fixed = lambda j, *_: (0, 0)
    out = lambda j, *_: (j, 0)
    body = functools.partial(head_body, tracks=tracks, first=first, which=which, scale=scale)
    return pl.pallas_call(
        body,
        grid_spec=pltpu.PrefetchScalarGridSpec(
            num_scalar_prefetch=2,
            grid=(tiles,),
            in_specs=[
                pl.BlockSpec((TILE, width), at),
                pl.BlockSpec((1, TILE), across),
                pl.BlockSpec((TILE * every, counts.shape[1]), at),
                pl.BlockSpec((tokens, width), fixed),
                pl.BlockSpec((width, tokens), fixed),
                pl.BlockSpec((width, tokens), fixed),
            ],
            out_specs=[
                pl.BlockSpec((TILE, width // 2), out),
                pl.BlockSpec((TILE, width // 2), out),
                pl.BlockSpec((width, tokens), fixed),
                pl.BlockSpec((1, TILE), lambda j, *_: (0, j)),
            ],
            scratch_shapes=[
                pltpu.VMEM((TILE, tokens), BF16),
                pltpu.VMEM((TILE, LANES), F32),
                pltpu.VMEM((TILE, counts.shape[1]), F32),
            ],
        ),
        out_shape=[
            jax.ShapeDtypeStruct((tiles * TILE, width // 2), BF16),
            jax.ShapeDtypeStruct((tiles * TILE, width // 2), BF16),
            jax.ShapeDtypeStruct((width, tokens), F32),
            jax.ShapeDtypeStruct((1, tiles * TILE), F32),
        ],
        compiler_params=pltpu.CompilerParams(vmem_limit_bytes=58 * 2**20),
        cost_estimate=pl.CostEstimate(
            flops=6 * tiles * TILE * width * tokens,
            bytes_accessed=tiles * TILE * (tokens * 4 + width * 4),
            transcendentals=3 * tiles * TILE * tokens,
        ),
    )(species, core, weight, bias, counts, rows, columns, before)


def finish_body(core_ref, mine_ref, other_ref, *rest):
    out_ref = rest[-1]
    half = mine_ref.shape[1]
    mine, other = mine_ref[...].astype(F32), other_ref[...].astype(F32)

    @pl.when(core_ref[0] == 0)
    def _():
        out_ref[:, :half] = mine
        out_ref[:, half:] = other

    @pl.when(core_ref[0] != 0)
    def _():
        out_ref[:, :half] = other
        out_ref[:, half:] = mine


def first_rows(tracks, width):
    return jax.ShapeDtypeStruct((tracks, width), F32)


def finish_head(shape, core, mine, other, first, earlier):
    rows, half = mine.shape
    tiles = min(rows // TILE, pl.cdiv(shape.shape[0], TILE) - first)
    half_spec = pl.BlockSpec((TILE, half), lambda j, *_: (j, 0))
    specs, values, aliases = [half_spec, half_spec], [mine, other], {}
    if earlier is not None:
        specs.append(pl.BlockSpec(memory_space=pl.ANY))
        values.append(earlier)
        aliases = {3: 0}
    return pl.pallas_call(
        finish_body,
        grid_spec=pltpu.PrefetchScalarGridSpec(
            num_scalar_prefetch=1,
            grid=(tiles,),
            in_specs=specs,
            out_specs=pl.BlockSpec((TILE, 2 * half), lambda j, *_: (first + j, 0)),
        ),
        out_shape=shape,
        input_output_aliases=aliases,
    )(core, *values)


def on_device(
    block_in,
    gain_in,
    shift_in,
    dilated_taps_weight,
    gain_mid,
    shift_mid,
    proj_weight,
    proj_bias,
    head_human,
    bias_human,
    head_mouse,
    bias_mouse,
    species,
    counts,
):
    windows, span, width = block_in.shape
    tokens = windows * span
    middle = proj_weight.shape[0]
    tracks_human = head_human.shape[1]
    tracks_mouse = head_mouse.shape[1]
    devices = lax.axis_size(EVERY)
    population = float(tokens * devices)
    core = lax.axis_index("core").astype(jnp.int32)[None]

    wide = block_in.reshape(tokens, width).astype(F32)
    sent, finish = small_sum([jnp.sum(wide, axis=0), jnp.sum(wide * wide, axis=0)])
    (before, after, everyone), _ = together(
        [*edges(block_in, DILATION_STEP), (sent, to_all)], lambda: (), ()
    )
    sum_in, square_in = finish(everyone)
    centre_in, scale_in = statistics(sum_in, square_in, population)

    def activate_in(values):
        return gelu_pair((values.astype(F32) - centre_in) * scale_in * gain_in + shift_in)

    normed_in = (wide - centre_in) * scale_in
    hidden_in, slope_in = gelu_pair(normed_in * gain_in + shift_in)
    hidden_in = hidden_in.astype(BF16).reshape(windows, span, width)
    place = lax.axis_index(BINS)
    last = lax.axis_size(BINS) - 1
    hidden_before = jnp.where(place > 0, activate_in(before)[0], 0.0).astype(BF16)
    hidden_after = jnp.where(place < last, activate_in(after)[0], 0.0).astype(BF16)
    padded = jnp.concatenate([hidden_before, hidden_in, hidden_after], axis=1)
    shifted = taps(padded, span)
    dilated = sum(
        jnp.dot(rows, dilated_taps_weight[k], preferred_element_type=F32)
        for k, rows in enumerate(shifted)
    )
    sent, finish = small_sum([jnp.sum(dilated, axis=0), jnp.sum(dilated * dilated, axis=0)])
    sum_mid, square_mid = finish(to_all(sent))
    centre_mid, scale_mid = statistics(sum_mid, square_mid, population)
    normed_mid = (dilated - centre_mid) * scale_mid
    hidden_mid, slope_mid = gelu_pair(normed_mid * gain_mid + shift_mid)
    hidden_mid = hidden_mid.astype(BF16)
    branch = jnp.dot(hidden_mid, proj_weight, preferred_element_type=F32)
    block_out = (wide + branch + proj_bias).astype(BF16)

    lane = min(span, LANES)
    counts_rows = (
        counts.transpose(2, 0, 1)
        .reshape(tracks_human, windows, span // lane, lane)
        .transpose(0, 2, 1, 3)
        .reshape(-1, lane)
    )
    columns = block_out.T
    tiles_human = pl.cdiv(tracks_human, TILE)
    tiles_mouse = pl.cdiv(tracks_mouse, TILE)
    cut = tiles_human // 3
    scale_human = math.sqrt(width / tracks_human)
    scale_mouse = math.sqrt(width / tracks_mouse)

    def human(first, tiles):
        def work(dy_t):
            return head(
                species, core, head_human.T, bias_human[None], counts_rows, block_out, columns,
                dy_t, first, tiles, 0, scale_human,
            )
        return work

    flat_x, flat_y, deep = bits_of("x"), bits_of("y"), bits_of("batch")
    near, far = deep[:1], deep[1:]
    start = jnp.zeros((width, tokens), F32)
    keep0, send0, dy_t, bias0 = head(
        species, core, head_mouse.T, bias_mouse[None], counts_rows, block_out, columns,
        start, 0, tiles_mouse, 1, scale_mouse,
    )
    (arrived0,), (keep1, send1, dy_t, bias1) = together(
        [(send0, lambda value: swap(value, CORE))], human(0, cut), (dy_t,)
    )
    first = Stream([keep0, arrived0], flat_x + near + flat_y + far)
    (arrived1,), (keep2, send2, dy_t, bias2) = advance(
        [first], [(send1, lambda value: swap(value, CORE))], human(cut, tiles_human - cut), (dy_t,)
    )
    second = Stream([keep1, arrived1], flat_y + flat_x + deep)

    def after_head(dy_t):
        output_grad = dy_t.T
        branch_grad = output_grad.astype(BF16)
        mid_grad = back_product(branch_grad, proj_weight) * slope_mid
        sent, _ = small_sum([jnp.sum(mid_grad, axis=0), jnp.sum(mid_grad * normed_mid, axis=0)])
        return output_grad, branch_grad, mid_grad, sent

    (arrived2,), (output_grad, branch_grad, mid_grad, sent) = advance(
        [first, second], [(send2, lambda value: swap(value, CORE))], after_head, (dy_t,)
    )
    unit = 16 * lax.axis_size(CHIPS)
    rows2 = keep2.shape[0]
    ends = [0] + [max(1, rows2 * (p + 1) // 3 // unit) * unit for p in range(2)] + [rows2]
    thirds = [
        Stream([keep2[low:high], arrived2[low:high]], route)
        for low, high, route in zip(
            ends[:-1],
            ends[1:],
            (flat_x + flat_y + deep, flat_y + near + flat_x + far, near + flat_x + flat_y + far),
        )
        if low < high
    ]
    streams = [first, second, *thirds]

    def weight_work(branch_grad, output_grad):
        return rows_product(branch_grad, hidden_mid), jnp.sum(output_grad, axis=0)

    (everyone,), (proj_grad, proj_bias_grad) = advance(
        streams, [(sent, to_all)], weight_work, (branch_grad, output_grad)
    )
    _, finish = small_sum([shift_mid, gain_mid])
    shift_mid_grad, gain_mid_grad = finish(everyone)
    dilated_grad = (
        scale_mid
        * gain_mid
        * (mid_grad - shift_mid_grad / population - normed_mid * gain_mid_grad / population)
    ).astype(BF16)

    def conv_work(dilated_grad, proj_grad):
        conv_grad = [rows_product(rows, dilated_grad) for rows in shifted]
        return jnp.concatenate([*conv_grad, proj_grad], axis=0).astype(BF16)

    dilated_windows = dilated_grad.reshape(windows, span, middle)
    (grad_before, grad_after), weights_grad = advance(
        streams, edges(dilated_windows, DILATION_STEP), conv_work, (dilated_grad, proj_grad)
    )

    def hidden_work(grad_before, dilated_windows, grad_after):
        grad_shifted = taps(
            jnp.concatenate([grad_before, dilated_windows, grad_after], axis=1), span
        )
        hidden_grad = sum(
            back_product(grad_shifted[2 - k], dilated_taps_weight[k]) for k in range(3)
        )
        in_grad = hidden_grad * slope_in
        sent, _ = small_sum([jnp.sum(in_grad, axis=0), jnp.sum(in_grad * normed_in, axis=0)])
        return in_grad, sent

    half = weights_grad.shape[0] // 2
    weights_keep = lax.dynamic_slice_in_dim(weights_grad, core[0] * half, half, 0)
    weights_send = lax.dynamic_slice_in_dim(weights_grad, (1 - core[0]) * half, half, 0)
    (arrived,), (in_grad, sent) = advance(
        streams,
        [(weights_send, lambda value: swap(value, CORE))],
        hidden_work,
        (grad_before, dilated_windows, grad_after),
    )
    chips = lax.axis_size(CHIPS)
    weights_half = (weights_keep.astype(F32) + arrived.astype(F32)).astype(BF16)
    weights_half = weights_half.reshape(chips, half // chips, middle)
    (everyone, weights_parts), _ = advance(
        streams, [(sent, to_all), (weights_half, lambda value: to_all(value, CHIPS))]
    )
    _, finish = small_sum([shift_in, gain_in])
    shift_in_grad, gain_in_grad = finish(everyone)

    def last_work(output_grad, in_grad):
        input_grad = output_grad + scale_in * gain_in * (
            in_grad - shift_in_grad / population - normed_in * gain_in_grad / population
        )
        return input_grad.astype(BF16)

    _, input_grad = advance(streams, [], last_work, (output_grad, in_grad))
    weights_share = jnp.sum(weights_parts.astype(F32), axis=0).astype(BF16)
    (weights_all,), _ = advance(
        streams,
        [
            (
                jnp.broadcast_to(weights_share[None], (chips,) + weights_share.shape),
                lambda value: to_all(value, CHIPS),
            )
        ],
    )
    weights_mine = weights_all.reshape(half, middle)
    sums = jnp.concatenate(
        [
            proj_bias_grad,
            bias1[0],
            bias2[0, : tracks_human - bias1.shape[1]],
            bias0[0, :tracks_mouse],
        ]
    )
    extra = [(weights_mine, lambda value: swap(value, CORE))]
    others = {}
    for stage in [stage for axis in EVERY for stage in bits_of(axis)]:
        ready = [s for s in (first, second) if not s.busy() and s not in others]
        moves = [(s.share, lambda value: swap(value, CORE)) for s in ready]
        got, _ = advance(
            streams,
            moves + extra + [(sums, functools.partial(lambda stage, value: swap(value, stage), stage))],
        )
        others.update(zip(ready, got))
        if extra:
            weights_other = got[len(ready)]
        extra = []
        sums = sums + got[-1]
    while any(stream.busy() for stream in streams):
        advance(streams)
    rest = [s for s in (first, second) if s not in others]
    mine2 = jnp.concatenate([s.share for s in thirds], axis=0)
    got, _ = advance(
        [], [(value, lambda value: swap(value, CORE)) for value in [mine2] + [s.share for s in rest]]
    )
    others.update(zip(rest, got[1:]))
    human_start = finish_head(first_rows(tracks_human, width), core, second.share, others[second], 0, None)
    head_human_grad = finish_head(
        first_rows(tracks_human, width), core, mine2, got[0], cut, human_start
    ).T
    head_mouse_grad = finish_head(
        first_rows(tracks_mouse, width), core, first.share, others[first], 0, None
    ).T
    left = jnp.where(core[0] == 0, weights_mine, weights_other).astype(F32)
    right = jnp.where(core[0] == 0, weights_other, weights_mine).astype(F32)
    weights_total = jnp.concatenate([left, right], axis=0)
    conv_total = weights_total[: 3 * width].reshape(3, width, middle)
    proj_total = weights_total[3 * width :].T
    return (
        block_out.reshape(windows, span, width),
        input_grad.reshape(windows, span, width),
        gain_in_grad,
        shift_in_grad,
        conv_total,
        gain_mid_grad,
        shift_mid_grad,
        proj_total,
        sums[:width],
        head_human_grad,
        sums[width : width + tracks_human],
        head_mouse_grad,
        sums[width + tracks_human :],
    )


def solution(mesh):
    bins, batch = mesh.shape["bins"], mesh.shape["batch"]
    side = 1 << (((bins // 2).bit_length() - 1) // 2)
    grid = jax.sharding.Mesh(
        mesh.devices.reshape(bins // 2 // side, side, 2, batch), ("y", "x", "core", "batch")
    )
    tokens = P("batch", BINS, None)
    placed = (tokens,) + (P(),) * 11 + (P("batch"), tokens)
    return jax.shard_map(
        on_device,
        mesh=grid,
        in_specs=placed,
        out_specs=(tokens, tokens) + (P(),) * 11,
        check_vma=False,
    )
```

profile of v0, /device:TPU:0, one launch (start us, length us, event | category | flops | bytes accessed | tf_op | source)
XLA Modules:
  0.0 478.7 jit_solution(17547669761126121265)
XLA Ops:
  3.6 7.3 %all-to-all-start = ((f32[32,1,1536]{2,1,0:T(1,128)}), f32[32,1,1536]{2,1,0:T(1,128)S(1)}, u32[]{:S(2)}, u32[]{:S(2)}) async-start(f32[32,1,1536]{2,1,0:T(1,128)} %all_to_all.34), calls=%async_computation | async-start | bytes 393216 | tf_op jit(solution)/shard_map/all_to_all | solution.py:45
  14.4 5.8 %all-to-all-done = f32[32,1,1536]{2,1,0:T(1,128)S(1)} async-done(((f32[32,1,1536]{2,1,0:T(1,128)}), f32[32,1,1536]{2,1,0:T(1,128)S(1)}, u32[]{:S(2)}, u32[]{:S(2)}) %all-to-all-start) | async-done | bytes 196640 | tf_op jit(solution)/shard_map/all_to_all | solution.py:45
  28.6 5.5 %all-to-all-start.1 = ((f32[32,1,768]{2,1,0:T(1,128)}), f32[32,1,768]{2,1,0:T(1,128)S(1)}, u32[]{:S(2)}, u32[]{:S(2)}) async-start(f32[32,1,768]{2,1,0:T(1,128)} %broadcast_in_dim.25), calls=%async_computation.1 | async-start | bytes 196608 | tf_op jit(solution)/shard_map/all_to_all | solution.py:45
  36.9 5.2 %all-to-all-done.1 = f32[32,1,768]{2,1,0:T(1,128)S(1)} async-done(((f32[32,1,768]{2,1,0:T(1,128)}), f32[32,1,768]{2,1,0:T(1,128)S(1)}, u32[]{:S(2)}, u32[]{:S(2)}) %all-to-all-start.1) | async-done | bytes 98336 | tf_op jit(solution)/shard_map/all_to_all | solution.py:45
  50.1 18.0 %shard_map.237 = (bf16[1792,384]{1,0:T(8,128)(2,1)}, bf16[1792,384]{1,0:T(8,128)(2,1)}, f32[768,1024]{1,0:T(8,128)}, f32[1,1792]{1,0:T(1,128)}) custom-call(s32[4]{0:T(128)} %species_ref.5, s32[1]{0:T(128)} %bitcast.8.core_ref, bf16[1643,768]{1,0:T(8,128)(2,1)} %bitcast.106, f32[1,1643]{1,0:T(1,128)} %broadcast_in_dim.27.bias_ref, s32[42504,128]{1,0:T(8,128)} %bitcast.79, ...), custom_call_target="tpu_custom_call" | custom-call | flops 8455716864 | bytes 12845056 | tf_op jit(solution)/shard_map/pallas_call | solution.py:279
  68.8 26.2 %shard_map.238 = (bf16[1792,384]{1,0:T(8,128)(2,1)}, bf16[1792,384]{1,0:T(8,128)(2,1)}, f32[768,1024]{1,0:T(8,128)}, f32[1,1792]{1,0:T(1,128)}) custom-call(s32[4]{0:T(128)} %species_ref.5, s32[1]{0:T(128)} %bitcast.8.core_ref, bf16[5313,768]{1,0:T(8,128)(2,1)} %bitcast.85, f32[1,5313]{1,0:T(1,128)} %broadcast_in_dim.29.bias_ref, s32[42504,128]{1,0:T(8,128)} %bitcast.80, ...), custom_call_target="tpu_custom_call" | custom-call | flops 8455716864 | bytes 12845056 | tf_op jit(solution)/shard_map/pallas_call | solution.py:279
  96.5 44.3 %shard_map.239 = (bf16[3584,384]{1,0:T(8,128)(2,1)}, bf16[3584,384]{1,0:T(8,128)(2,1)}, f32[768,1024]{1,0:T(8,128)}, f32[1,3584]{1,0:T(1,128)}) custom-call(s32[4]{0:T(128)} %species_ref.5, s32[1]{0:T(128)} %bitcast.8.core_ref, bf16[5313,768]{1,0:T(8,128)(2,1)} %bitcast.86, f32[1,5313]{1,0:T(1,128)} %broadcast_in_dim.29.bias_ref, s32[42504,128]{1,0:T(8,128)} %bitcast.81, ...), custom_call_target="tpu_custom_call" | custom-call | flops 16911433728 | bytes 25690112 | tf_op jit(solution)/shard_map/pallas_call | solution.py:279
  150.1 10.0 %collective-permute-done.5 = bf16[448,384]{1,0:T(8,128)(2,1)S(1)} collective-permute-done((bf16[448,384]{1,0:T(8,128)(2,1)S(1)}, bf16[448,384]{1,0:T(8,128)(2,1)S(1)}, u32[]{:S(2)}, u32[]{:S(2)}) %collective-permute-start.5) | collective-permute-done | bytes 344096 | tf_op jit(solution)/shard_map/ppermute | solution.py:51
  172.0 4.1 all-to-all-start.2
  182.7 6.6 %all-to-all-done.2 = f32[32,1,768]{2,1,0:T(1,128)S(1)} async-done(((f32[32,1,768]{2,1,0:T(1,128)}), f32[32,1,768]{2,1,0:T(1,128)S(1)}, u32[]{:S(2)}, u32[]{:S(2)}) %all-to-all-start.2) | async-done | bytes 98336 | tf_op jit(solution)/shard_map/all_to_all | solution.py:45
  214.8 5.2 %collective-permute-done.13 = bf16[112,384]{1,0:T(8,128)(2,1)S(1)} collective-permute-done((bf16[112,384]{1,0:T(8,128)(2,1)S(1)}, bf16[112,384]{1,0:T(8,128)(2,1)S(1)}, u32[]{:S(2)}, u32[]{:S(2)}) %collective-permute-start.13) | collective-permute-done | bytes 86048 | tf_op jit(solution)/shard_map/ppermute | solution.py:51
  238.9 4.2 collective-permute-done.21
  251.1 14.1 %all_to_all.52 = f32[32,1,1536]{2,1,0:T(1,128)S(1)} all-to-all(f32[32,1,1536]{2,1,0:T(1,128)S(1)} %all_to_all.41), channel_id=1, replica_groups=mesh['y'=2,'x'=2,'core'=2,'batch'=4] {'y','x','core','batch'}, dimensions={0} | all-to-all | bytes 393216 | tf_op jit(solution)/shard_map/all_to_all | solution.py:45
  265.2 4.4 all-to-all-start.4
  277.9 31.5 %collective-permute-done.28 = bf16[64,384]{1,0:T(8,128)(2,1)} collective-permute-done((bf16[64,384]{1,0:T(8,128)(2,1)}, bf16[64,384]{1,0:T(8,128)(2,1)}, u32[]{:S(2)}, u32[]{:S(2)}) %collective-permute-start.28) | collective-permute-done | bytes 49184 | tf_op jit(solution)/shard_map/ppermute | solution.py:51
  325.2 4.4 add_convert_fusion
  346.2 5.9 %all-to-all-start.5 = ((bf16[16,96,384]{2,1,0:T(8,128)(2,1)}), bf16[16,96,384]{2,1,0:T(8,128)(2,1)S(1)}, u32[]{:S(2)}, u32[]{:S(2)}) async-start(bf16[16,96,384]{2,1,0:T(8,128)(2,1)} %broadcast_in_dim.32), calls=%async_computation.5 | async-start | bytes 2359296 | tf_op jit(solution)/shard_map/all_to_all | solution.py:45
  362.5 10.6 %collective-permute-done.38 = bf16[128,384]{1,0:T(8,128)(2,1)} collective-permute-done((bf16[128,384]{1,0:T(8,128)(2,1)}, bf16[128,384]{1,0:T(8,128)(2,1)}, u32[]{:S(2)}, u32[]{:S(2)}) %collective-permute-start.38) | collective-permute-done | bytes 98336 | tf_op jit(solution)/shard_map/ppermute | solution.py:51
  373.0 18.1 %collective-permute-done.39 = bf16[160,384]{1,0:T(8,128)(2,1)} collective-permute-done((bf16[160,384]{1,0:T(8,128)(2,1)}, bf16[160,384]{1,0:T(8,128)(2,1)}, u32[]{:S(2)}, u32[]{:S(2)}) %collective-permute-start.39) | collective-permute-done | bytes 122912 | tf_op jit(solution)/shard_map/ppermute | solution.py:51
  399.0 18.8 %collective-permute-done.47 = f32[7724]{0:T(1024)S(1)} collective-permute-done((f32[7724]{0:T(1024)S(1)}, f32[7724]{0:T(1024)S(1)}, u32[]{:S(2)}, u32[]{:S(2)}) %collective-permute-start.47) | collective-permute-done | bytes 30928 | tf_op jit(solution)/shard_map/ppermute | solution.py:51
  419.9 5.1 %collective-permute-done.43 = bf16[320,384]{1,0:T(8,128)(2,1)S(1)} collective-permute-done((bf16[320,384]{1,0:T(8,128)(2,1)S(1)}, bf16[320,384]{1,0:T(8,128)(2,1)S(1)}, u32[]{:S(2)}, u32[]{:S(2)}) %collective-permute-start.43) | collective-permute-done | bytes 245792 | tf_op jit(solution)/shard_map/ppermute | solution.py:51
  432.3 9.6 %collective-permute-done.52 = f32[7724]{0:T(1024)S(1)} collective-permute-done((f32[7724]{0:T(1024)S(1)}, f32[7724]{0:T(1024)S(1)}, u32[]{:S(2)}, u32[]{:S(2)}) %collective-permute-start.52) | collective-permute-done | bytes 30928 | tf_op jit(solution)/shard_map/ppermute | solution.py:51
  465.2 4.0 shard_map.240.rest_0_
  471.1 7.4 %shard_map.241 = f32[5313,768]{1,0:T(8,128)} custom-call(s32[1]{0:T(128)} %bitcast.8.core_ref, bf16[3584,384]{1,0:T(8,128)(2,1)} %select_dynamic-update-slice_fusion.mine_ref, bf16[3584,384]{1,0:T(8,128)(2,1)} %collective-permute-done.56.other_ref, f32[5313,768]{1,0:T(8,128)} %shard_map.240.rest_0_), custom_call_target="tpu_custom_call", output_to_operand_aliasing={{}: (3, {})} | custom-call | tf_op jit(solution)/shard_map/pallas_call | solution.py:348
  (392 shorter events, 200.4 us)
Async XLA Ops:
  68.1 27.0 %collective-permute-start.2 = (bf16[1792,384]{1,0:T(8,128)(2,1)}, bf16[1792,384]{1,0:T(8,128)(2,1)S(1)}, u32[]{:S(2)}, u32[]{:S(2)}) collective-permute-start(bf16[1792,384]{1,0:T(8,128)(2,1)} %get-tuple-element.180), channel_id=1, source_target_pairs={{0,4},{4,0},{1,5},{5,1},{2,6},{6,2},{3,7},{7,3},{8,12},{12,8},{9,1... | collective-permute-start | bytes 4128776 | tf_op jit(solution)/shard_map/ppermute | solution.py:51
  95.3 45.6 %collective-permute-start.4 = (bf16[1792,384]{1,0:T(8,128)(2,1)}, bf16[1792,384]{1,0:T(8,128)(2,1)S(1)}, u32[]{:S(2)}, u32[]{:S(2)}) collective-permute-start(bf16[1792,384]{1,0:T(8,128)(2,1)} %get-tuple-element.190), channel_id=1, source_target_pairs={{0,4},{4,0},{1,5},{5,1},{2,6},{6,2},{3,7},{7,3},{8,12},{12,8},{9,1... | collective-permute-start | bytes 4128776 | tf_op jit(solution)/shard_map/ppermute | solution.py:51
  95.8 45.0 %collective-permute-start.3 = (bf16[896,384]{1,0:T(8,128)(2,1)S(1)}, bf16[896,384]{1,0:T(8,128)(2,1)}, u32[]{:S(2)}, u32[]{:S(2)}) collective-permute-start(bf16[896,384]{1,0:T(8,128)(2,1)S(1)} %add_convert_fusion.4), channel_id=1, source_target_pairs={{0,8},{8,0},{1,9},{9,1},{2,10},{10,2},{3,11},{11,3},{4,12},{12,4},... | collective-permute-start | bytes 2064392 | tf_op jit(solution)/shard_map/ppermute | solution.py:51
  168.7 20.7 %collective-permute-start.11 = (bf16[640,384]{1,0:T(8,128)(2,1)}, bf16[640,384]{1,0:T(8,128)(2,1)}, u32[]{:S(2)}, u32[]{:S(2)}) collective-permute-start(bf16[640,384]{1,0:T(8,128)(2,1)} %add_convert_fusion.6), channel_id=1, source_target_pairs={{0,16},{16,0},{1,17},{17,1},{2,18},{18,2},{3,19},{19,3},{4,20},{20... | collective-permute-start | bytes 1474568 | tf_op jit(solution)/shard_map/ppermute | solution.py:51
  169.3 20.1 %collective-permute-start.12 = (bf16[640,384]{1,0:T(8,128)(2,1)}, bf16[640,384]{1,0:T(8,128)(2,1)}, u32[]{:S(2)}, u32[]{:S(2)}) collective-permute-start(bf16[640,384]{1,0:T(8,128)(2,1)} %add_convert_fusion.5), channel_id=1, source_target_pairs={{0,1},{1,0},{2,3},{3,2},{4,5},{5,4},{6,7},{7,6},{8,9},{9,8},{10,11... | collective-permute-start | bytes 1474568 | tf_op jit(solution)/shard_map/ppermute | solution.py:51
  169.3 20.1 %collective-permute-start.10 = (bf16[512,384]{1,0:T(8,128)(2,1)}, bf16[512,384]{1,0:T(8,128)(2,1)}, u32[]{:S(2)}, u32[]{:S(2)}) collective-permute-start(bf16[512,384]{1,0:T(8,128)(2,1)} %add_convert_fusion.7), channel_id=1, source_target_pairs={{0,8},{8,0},{1,9},{9,1},{2,10},{10,2},{3,11},{11,3},{4,12},{12,4},... | collective-permute-start | bytes 1179656 | tf_op jit(solution)/shard_map/ppermute | solution.py:51
  170.8 18.5 %collective-permute-start.9 = (bf16[448,384]{1,0:T(8,128)(2,1)}, bf16[448,384]{1,0:T(8,128)(2,1)}, u32[]{:S(2)}, u32[]{:S(2)}) collective-permute-start(bf16[448,384]{1,0:T(8,128)(2,1)} %add_convert_fusion.8), channel_id=1, source_target_pairs={{0,8},{8,0},{1,9},{9,1},{2,10},{10,2},{3,11},{11,3},{4,12},{12,4},... | collective-permute-start | bytes 1032200 | tf_op jit(solution)/shard_map/ppermute | solution.py:51
  265.2 44.3 %all-to-all-start.4 = ((bf16[16,96,384]{2,1,0:T(8,128)(2,1)}), bf16[16,96,384]{2,1,0:T(8,128)(2,1)}, u32[]{:S(2)}, u32[]{:S(2)}) async-start(bf16[16,96,384]{2,1,0:T(8,128)(2,1)} %bitcast.97), calls=%async_computation.4 | async-start | bytes 2359296 | tf_op jit(solution)/shard_map/all_to_all | solution.py:45
  269.6 39.9 %collective-permute-start.26 = (bf16[224,384]{1,0:T(8,128)(2,1)}, bf16[224,384]{1,0:T(8,128)(2,1)}, u32[]{:S(2)}, u32[]{:S(2)}) collective-permute-start(bf16[224,384]{1,0:T(8,128)(2,1)} %pad_maximum_fusion.18), channel_id=1, source_target_pairs={{0,16},{16,0},{1,17},{17,1},{2,18},{18,2},{3,19},{19,3},{4,20},{20... | collective-permute-start | bytes 516104 | tf_op jit(solution)/shard_map/ppermute | solution.py:51
  271.4 38.1 %collective-permute-start.27 = (bf16[112,384]{1,0:T(8,128)(2,1)S(1)}, bf16[112,384]{1,0:T(8,128)(2,1)S(1)}, u32[]{:S(2)}, u32[]{:S(2)}) collective-permute-start(bf16[112,384]{1,0:T(8,128)(2,1)S(1)} %add_convert_fusion.18), channel_id=1, source_target_pairs={{0,2},{1,3},{2,0},{3,1},{4,6},{5,7},{6,4},{7,5},{8,10},{9,11},{10,... | collective-permute-start | bytes 258056 | tf_op jit(solution)/shard_map/ppermute | solution.py:51
  273.8 35.7 %collective-permute-start.29 = (bf16[80,384]{1,0:T(8,128)(2,1)}, bf16[80,384]{1,0:T(8,128)(2,1)}, u32[]{:S(2)}, u32[]{:S(2)}) collective-permute-start(bf16[80,384]{1,0:T(8,128)(2,1)} %add_convert_fusion.25), channel_id=1, source_target_pairs={{0,2},{1,3},{2,0},{3,1},{4,6},{5,7},{6,4},{7,5},{8,10},{9,11},{10,... | collective-permute-start | bytes 184328 | tf_op jit(solution)/shard_map/ppermute | solution.py:51
  274.3 35.1 %collective-permute-start.30 = (bf16[80,384]{1,0:T(8,128)(2,1)}, bf16[80,384]{1,0:T(8,128)(2,1)}, u32[]{:S(2)}, u32[]{:S(2)}) collective-permute-start(bf16[80,384]{1,0:T(8,128)(2,1)} %add_convert_fusion.24), channel_id=1, source_target_pairs={{0,2},{1,3},{2,0},{3,1},{4,6},{5,7},{6,4},{7,5},{8,10},{9,11},{10,... | collective-permute-start | bytes 184328 | tf_op jit(solution)/shard_map/ppermute | solution.py:51
  276.7 32.8 %collective-permute-start.28 = (bf16[64,384]{1,0:T(8,128)(2,1)}, bf16[64,384]{1,0:T(8,128)(2,1)}, u32[]{:S(2)}, u32[]{:S(2)}) collective-permute-start(bf16[64,384]{1,0:T(8,128)(2,1)} %add_convert_fusion.27), channel_id=1, source_target_pairs={{0,2},{1,3},{2,0},{3,1},{4,6},{5,7},{6,4},{7,5},{8,10},{9,11},{10,... | collective-permute-start | bytes 147464 | tf_op jit(solution)/shard_map/ppermute | solution.py:51
  346.2 44.9 %all-to-all-start.5 = ((bf16[16,96,384]{2,1,0:T(8,128)(2,1)}), bf16[16,96,384]{2,1,0:T(8,128)(2,1)S(1)}, u32[]{:S(2)}, u32[]{:S(2)}) async-start(bf16[16,96,384]{2,1,0:T(8,128)(2,1)} %broadcast_in_dim.32), calls=%async_computation.5 | async-start | bytes 2359296 | tf_op jit(solution)/shard_map/all_to_all | solution.py:45
  352.0 39.1 %collective-permute-start.36 = (bf16[896,384]{1,0:T(8,128)(2,1)}, bf16[896,384]{1,0:T(8,128)(2,1)S(1)}, u32[]{:S(2)}, u32[]{:S(2)}) collective-permute-start(bf16[896,384]{1,0:T(8,128)(2,1)} %pad_maximum_fusion.8), channel_id=1, source_target_pairs={{0,8},{8,0},{1,9},{9,1},{2,10},{10,2},{3,11},{11,3},{4,12},{12,4},... | collective-permute-start | bytes 2064392 | tf_op jit(solution)/shard_map/ppermute | solution.py:51
  354.1 37.0 %collective-permute-start.37 = (bf16[448,384]{1,0:T(8,128)(2,1)}, bf16[448,384]{1,0:T(8,128)(2,1)S(1)}, u32[]{:S(2)}, u32[]{:S(2)}) collective-permute-start(bf16[448,384]{1,0:T(8,128)(2,1)} %pad_maximum_fusion.14), channel_id=1, source_target_pairs={{0,8},{8,0},{1,9},{9,1},{2,10},{10,2},{3,11},{11,3},{4,12},{12,4},... | collective-permute-start | bytes 1032200 | tf_op jit(solution)/shard_map/ppermute | solution.py:51
  354.2 36.9 %collective-permute-start.39 = (bf16[160,384]{1,0:T(8,128)(2,1)}, bf16[160,384]{1,0:T(8,128)(2,1)}, u32[]{:S(2)}, u32[]{:S(2)}) collective-permute-start(bf16[160,384]{1,0:T(8,128)(2,1)} %pad_maximum_fusion.20), channel_id=1, source_target_pairs={{0,8},{8,0},{1,9},{9,1},{2,10},{10,2},{3,11},{11,3},{4,12},{12,4},... | collective-permute-start | bytes 368648 | tf_op jit(solution)/shard_map/ppermute | solution.py:51
  356.2 35.0 %collective-permute-start.40 = (bf16[160,384]{1,0:T(8,128)(2,1)}, bf16[160,384]{1,0:T(8,128)(2,1)}, u32[]{:S(2)}, u32[]{:S(2)}) collective-permute-start(bf16[160,384]{1,0:T(8,128)(2,1)} %pad_maximum_fusion.21), channel_id=1, source_target_pairs={{0,16},{16,0},{1,17},{17,1},{2,18},{18,2},{3,19},{19,3},{4,20},{20... | collective-permute-start | bytes 368648 | tf_op jit(solution)/shard_map/ppermute | solution.py:51
  394.9 32.2 %collective-permute-start.45 = (bf16[1792,384]{1,0:T(8,128)(2,1)S(1)}, bf16[1792,384]{1,0:T(8,128)(2,1)}, u32[]{:S(2)}, u32[]{:S(2)}) collective-permute-start(bf16[1792,384]{1,0:T(8,128)(2,1)S(1)} %pad_maximum_fusion.4.mine_ref), channel_id=1, source_target_pairs={{0,4},{4,0},{1,5},{5,1},{2,6},{6,2},{3,7},{7,3},{8,12},{12,8},{9,1... | collective-permute-start | bytes 4128776 | tf_op jit(solution)/shard_map/ppermute | solution.py:51
  395.0 31.1 %collective-permute-start.46 = (bf16[1536,384]{1,0:T(8,128)(2,1)S(1)}, bf16[1536,384]{1,0:T(8,128)(2,1)S(1)}, u32[]{:S(2)}, u32[]{:S(2)}) collective-permute-start(bf16[1536,384]{1,0:T(8,128)(2,1)S(1)} %bitcast.96), channel_id=1, source_target_pairs={{0,4},{4,0},{1,5},{5,1},{2,6},{6,2},{3,7},{7,3},{8,12},{12,8},{9,1... | collective-permute-start | bytes 3538952 | tf_op jit(solution)/shard_map/ppermute | solution.py:51
  395.5 30.6 %collective-permute-start.41 = (bf16[896,384]{1,0:T(8,128)(2,1)S(1)}, bf16[896,384]{1,0:T(8,128)(2,1)S(1)}, u32[]{:S(2)}, u32[]{:S(2)}) collective-permute-start(bf16[896,384]{1,0:T(8,128)(2,1)S(1)} %pad_maximum_fusion.9), channel_id=1, source_target_pairs={{0,16},{16,0},{1,17},{17,1},{2,18},{18,2},{3,19},{19,3},{4,20},{20... | collective-permute-start | bytes 2064392 | tf_op jit(solution)/shard_map/ppermute | solution.py:51
  397.0 22.3 %collective-permute-start.42 = (bf16[256,384]{1,0:T(8,128)(2,1)S(1)}, bf16[256,384]{1,0:T(8,128)(2,1)S(1)}, u32[]{:S(2)}, u32[]{:S(2)}) collective-permute-start(bf16[256,384]{1,0:T(8,128)(2,1)S(1)} %pad_maximum_fusion.17), channel_id=1, source_target_pairs={{0,16},{16,0},{1,17},{17,1},{2,18},{18,2},{3,19},{19,3},{4,20},{20... | collective-permute-start | bytes 589832 | tf_op jit(solution)/shard_map/ppermute | solution.py:51
  397.5 20.3 %collective-permute-start.47 = (f32[7724]{0:T(1024)S(1)}, f32[7724]{0:T(1024)S(1)}, u32[]{:S(2)}, u32[]{:S(2)}) collective-permute-start(f32[7724]{0:T(1024)S(1)} %copy-done.50), channel_id=1, source_target_pairs={{0,16},{16,0},{1,17},{17,1},{2,18},{18,2},{3,19},{19,3},{4,20},{20... | collective-permute-start | bytes 92696 | tf_op jit(solution)/shard_map/ppermute | solution.py:51
  448.4 22.7 %collective-permute-start.56 = (bf16[3584,384]{1,0:T(8,128)(2,1)}, bf16[3584,384]{1,0:T(8,128)(2,1)}, u32[]{:S(2)}, u32[]{:S(2)}) collective-permute-start(bf16[3584,384]{1,0:T(8,128)(2,1)} %select_dynamic-update-slice_fusion.mine_ref), channel_id=1, source_target_pairs={{0,4},{4,0},{1,5},{5,1},{2,6},{6,2},{3,7},{7,3},{8,12},{12,8},{9,1... | collective-permute-start | bytes 8257544 | tf_op jit(solution)/shard_map/ppermute | solution.py:51
  (111 other events, 1531.7 us)
where the time goes:
time: 486 us; the launch traced here: 479 us
  waiting for transfers between devices  146 us (30%)
  Pallas kernels  104 us (21%)
  starting transfers between devices  88.3 us (18%)
  other arithmetic  77.2 us (16%)
  matrix products  24.1 us (5%)
  local copies, waits for them, and re-layouts  23.4 us (5%)
  blocking collectives  14.1 us (3%)
    ppermute x53, waiting for transfers between devices, swap(): return lax.ppermute(value, axis, [(i, i ^ mask) for i in range(size)])  128 us
    pallas_call x3, Pallas kernels, head(): pl.pallas_call(body, grid_spec=pltpu.PrefetchScalarGridSpec(num_scalar_pr...  88.6 us
    ppermute x53, starting transfers between devices, swap(): return lax.ppermute(value, axis, [(i, i ^ mask) for i in range(size)])  54.4 us
    convert_element_type x23, other arithmetic, part(): return sum((lax.dynamic_slice_in_dim(piece, at + which * self.rows, self....  29.5 us
    all_to_all x5, starting transfers between devices, to_all(): return lax.all_to_all(sent, axes, 0, 0, tiled=True)  27.1 us
    all_to_all x5, waiting for transfers between devices, to_all(): return lax.all_to_all(sent, axes, 0, 0, tiled=True)  17.6 us
    pallas_call x3, Pallas kernels, finish_head(): pl.pallas_call(finish_body, grid_spec=pltpu.PrefetchScalarGridSpec(num_sc...  15.3 us
    all_to_all x1, blocking collectives, to_all(): return lax.all_to_all(sent, axes, 0, 0, tiled=True)  14.1 us
  transfers between devices with their start and end apart: 62, of which 21 were waited for; matrix products, arithmetic and copies ran while one was open for 8% of the time, Pallas kernels for 16%

commit v1 on v0

v1 whole, which is shorter than its diff:
```python
import functools
import math

import jax
import jax.numpy as jnp
from jax import lax
from jax.experimental import pallas as pl
from jax.experimental.pallas import tpu as pltpu
from jax.sharding import PartitionSpec as P

DILATION_STEP = 11
EPS = 1e-05
F32 = jnp.float32
BF16 = jnp.bfloat16
EVERY = ("y", "x", "core", "batch")
BINS = ("y", "x", "core")
CHIPS = ("y", "x", "batch")
CORE = ("core", 1)
LANES = 128
TILE = 896


def bits_of(axis):
    return [(axis, 1 << i) for i in range(lax.axis_size(axis).bit_length() - 1)]


def small_sum(parts):
    flat = jnp.concatenate([part.reshape(-1) for part in parts])
    peers = lax.axis_size(EVERY)
    sent = jnp.broadcast_to(flat[None], (peers, flat.shape[0]))
    cuts = [part.size for part in parts]

    def finish(everyone):
        total = jnp.sum(everyone, axis=0)
        ends = [sum(cuts[: i + 1]) for i in range(len(cuts))]
        return [
            total[end - cut : end].reshape(part.shape)
            for part, cut, end in zip(parts, cuts, ends)
        ]

    return sent, finish


def to_all(sent, axes=EVERY):
    return lax.all_to_all(sent, axes, 0, 0, tiled=True)


def swap(value, stage):
    axis, mask = stage
    size = lax.axis_size(axis)
    return lax.ppermute(value, axis, [(i, i ^ mask) for i in range(size)])


def upper(stage):
    axis, mask = stage
    return ((lax.axis_index(axis) & mask) != 0).astype(jnp.int32)


def sum_body(at_ref, *refs, counts):
    ins, outs = refs[: sum(counts)], refs[sum(counts) :]
    used = 0
    for out, count in zip(outs, counts):
        total = sum(ref[...].astype(F32) for ref in ins[used : used + count])
        out[...] = total.astype(out.dtype)
        used += count


def sum_parts(parts, dtype):
    if any(rows % 16 for rows, _ in parts):
        sums = [
            sum(lax.dynamic_slice_in_dim(a, at, rows, 0).astype(F32) for a, at in pieces)
            for rows, pieces in parts
        ]
        return [value.astype(dtype) for value in sums]
    lanes = parts[0][1][0][0].shape[1]
    places, specs, values, counts, shapes = [], [], [], [], []
    for rows, pieces in parts:
        for array, at in pieces:
            specs.append(
                pl.BlockSpec((rows, lanes), lambda j, at_ref, i=len(places): (at_ref[i], 0))
            )
            places.append(jnp.asarray(at, jnp.int32) // rows)
            values.append(array)
        counts.append(len(pieces))
        shapes.append(rows)
    return pl.pallas_call(
        functools.partial(sum_body, counts=counts),
        grid_spec=pltpu.PrefetchScalarGridSpec(
            num_scalar_prefetch=1,
            grid=(1,),
            in_specs=specs,
            out_specs=[pl.BlockSpec((rows, lanes), lambda j, *_: (0, 0)) for rows in shapes],
        ),
        out_shape=[jax.ShapeDtypeStruct((rows, lanes), dtype) for rows in shapes],
        compiler_params=pltpu.CompilerParams(vmem_limit_bytes=60 * 2**20),
    )(jnp.stack(places), *values)


def join_body(mine_ref, *refs, count, stacked):
    row = 0
    for i in range(count):
        share, arrived = refs[2 * i], refs[2 * i + 1]
        out = refs[2 * count + (0 if stacked else i)]
        rows = share.shape[0]
        mine = mine_ref[i]
        out[pl.ds(pl.multiple_of(row + mine * rows, 16), rows), :] = share[...]
        out[pl.ds(pl.multiple_of(row + (1 - mine) * rows, 16), rows), :] = arrived[...]
        if stacked:
            row += 2 * rows


def join_parts(parts, stacked=False):
    if any(share.shape[0] % 16 for share, _, _ in parts):
        joined = [
            jnp.concatenate([jnp.where(mine == 1, b, a), jnp.where(mine == 1, a, b)], axis=0)
            for a, b, mine in parts
        ]
        return [jnp.concatenate(joined, axis=0)] if stacked else joined
    outs = [2 * a.shape[0] for a, _, _ in parts]
    if stacked:
        outs = [sum(outs)]
    lanes = parts[0][0].shape[1]
    whole = lambda rows: pl.BlockSpec((rows, lanes), lambda j, *_: (0, 0))
    return pl.pallas_call(
        functools.partial(join_body, count=len(parts), stacked=stacked),
        grid_spec=pltpu.PrefetchScalarGridSpec(
            num_scalar_prefetch=1,
            grid=(1,),
            in_specs=[whole(v.shape[0]) for a, b, _ in parts for v in (a, b)],
            out_specs=[whole(rows) for rows in outs],
        ),
        out_shape=[jax.ShapeDtypeStruct((rows, lanes), BF16) for rows in outs],
        compiler_params=pltpu.CompilerParams(vmem_limit_bytes=60 * 2**20),
    )(jnp.stack([mine for _, _, mine in parts]), *[v for a, b, _ in parts for v in (a, b)])


class Group:
    def __init__(self, order, pieces, rows, base, routes):
        self.order = order
        self.parts = [
            {"pieces": [(piece, at + base) for piece in pieces], "rows": count, "route": route}
            for at, count, route in zip(
                [sum(rows[:i]) for i in range(len(rows))], rows, routes
            )
        ]
        self.levels = len(routes[0])
        self.level = 0
        self.flying = None
        self.shares = None

    def moved(self, values, level):
        self.flying = [
            swap(value, part["route"][level]) for value, part in zip(values, self.parts)
        ]

    def work(self, arrays, flying):
        level = self.level
        parts = self.parts
        if level <= self.levels:
            wanted = []
            for i, part in enumerate(parts):
                pieces = list(zip(arrays[i], [at for _, at in part["pieces"]]))
                if level:
                    mine = upper(part["route"][level - 1])
                    pieces = [(a, at + mine * part["rows"]) for a, at in pieces]
                    pieces.append((flying[i], 0))
                part["pieces"] = pieces
                if level < self.levels:
                    part["rows"] //= 2
                    away = 1 - upper(part["route"][level])
                    pieces = [(a, at + away * part["rows"]) for a, at in pieces]
                wanted.append((part["rows"], pieces))
            return sum_parts(wanted, F32 if level < self.levels else BF16)
        back = 2 * self.levels - level
        return join_parts(
            [
                (share, arrived, upper(part["route"][back]))
                for share, arrived, part in zip(self.shares, flying, parts)
            ],
            stacked=level == 2 * self.levels,
        )

    def step(self):
        if self.done():
            return
        arrays = [[a for a, _ in part["pieces"]] for part in self.parts]
        values = self.order.run(self.work, arrays, self.flying)
        if self.level >= self.levels:
            self.shares = values
        if self.level < self.levels:
            self.moved(values, self.level)
        elif self.level < 2 * self.levels:
            self.moved(values, 2 * self.levels - 1 - self.level)
        self.level += 1

    def done(self):
        return self.level > 2 * self.levels


class Order:
    def __init__(self):
        self.token = ()

    def run(self, work, *given):
        given, _ = lax.optimization_barrier((given, self.token))
        result = work(*given)
        self.token = jax.tree.leaves(result)[:1]
        return result


def gelu_pair(values):
    logistic = jax.nn.sigmoid(1.702 * values)
    return (values * logistic, logistic + 1.702 * values * logistic * (1.0 - logistic))


def rows_product(former, latter):
    return lax.dot_general(
        former, latter, (((0,), (0,)), ((), ())), preferred_element_type=F32
    )


def back_product(former, latter):
    return lax.dot_general(
        former, latter, (((1,), (1,)), ((), ())), preferred_element_type=F32
    )


def taps(padded_rows, span):
    windows = padded_rows.shape[0]
    return [
        padded_rows[:, k * DILATION_STEP : k * DILATION_STEP + span, :].reshape(
            windows * span, -1
        )
        for k in range(3)
    ]


def statistics(plain_sum, square_sum, population):
    centre = plain_sum / population
    return (centre, lax.rsqrt(square_sum / population - centre * centre + EPS))


def edges(shard, width):
    peers, length = (lax.axis_size(BINS), shard.shape[1])
    up = [(i, i + 1) for i in range(peers - 1)]
    down = [(i + 1, i) for i in range(peers - 1)]
    return (
        (shard[:, length - width :], lambda value: lax.ppermute(value, BINS, up)),
        (shard[:, :width], lambda value: lax.ppermute(value, BINS, down)),
    )


def poisson_slope(logits, counted):
    held = jnp.maximum(logits, -80.0)
    small = jnp.exp(-jnp.abs(held))
    whole = 1.0 + small
    tail = jnp.where(small < 1e-3, small * (1.0 - 0.5 * small), jnp.log(whole))
    rate = jnp.maximum(held, 0.0) + tail
    top = jnp.where(held >= 0.0, 1.0, small)
    return top * (rate - counted) / (whole * rate)


def head_body(
    species_ref,
    windows_ref,
    humans_ref,
    core_ref,
    mouse_ref,
    human_ref,
    bias_mouse_ref,
    bias_human_ref,
    counts_ref,
    rows_ref,
    columns_ref,
    *refs,
    mouse_tiles,
    first_human,
    tracks,
    scales,
):
    *out_refs, grads_ref, bias_grad_ref, weight_ref, bias_ref, sums_ref, total_ref = refs
    step = pl.program_id(0)
    tile, width = weight_ref.shape
    windows = windows_ref.shape[0]
    span = rows_ref.shape[0] // windows
    lane = counts_ref.shape[1]
    groups = span // lane
    half = width // 2
    is_mouse = step < mouse_tiles
    humans = humans_ref[0]
    active = jnp.where(is_mouse, windows - humans, humans)
    skipped = jnp.where(is_mouse, humans, 0)
    first = jnp.where(is_mouse, step, first_human + step - mouse_tiles) * tile
    end = jnp.where(is_mouse, tracks[1], tracks[0])
    scale = jnp.where(is_mouse, scales[1], scales[0]).astype(F32)

    def prepare():
        inside = first + lax.broadcasted_iota(jnp.int32, (tile, 1), 0) < end

        @pl.when(is_mouse)
        def _():
            weight_ref[...] = jnp.where(inside, mouse_ref[...], BF16(0))
            bias_ref[...] = jnp.broadcast_to(bias_mouse_ref[...], (LANES, tile)).T

        @pl.when(jnp.logical_not(is_mouse))
        def _():
            weight_ref[...] = jnp.where(inside, human_ref[...], BF16(0))
            bias_ref[...] = jnp.broadcast_to(bias_human_ref[...], (LANES, tile)).T

    def slopes(logits, window):
        inside = first + lax.broadcasted_iota(jnp.int32, (tile, 1), 0) < end
        total = jnp.zeros((tile, lane), F32)
        low = []
        for h in range(groups):
            counted = counts_ref[
                pl.ds(h * windows + window, tile, stride=groups * windows), :
            ].astype(F32)
            part = logits[:, h * lane : (h + 1) * lane] + bias_ref[:, :lane]
            slope = jnp.where(inside, poisson_slope(part, counted) * scale, 0.0)
            total = total + slope
            low.append(slope.astype(BF16))
        return total, jnp.concatenate(low, axis=1)

    def store(product):
        if len(out_refs) == 1:
            out_refs[0][...] = product
            return
        mine = core_ref[0] == 0
        out_refs[0][...] = jnp.where(mine, product[:, :half], product[:, half:])
        out_refs[1][...] = jnp.where(mine, product[:, half:], product[:, :half])

    @pl.when(active == 0)
    def _():
        for out_ref in out_refs:
            out_ref[...] = jnp.zeros_like(out_ref)
        grads_ref[...] = jnp.zeros_like(grads_ref)
        bias_grad_ref[...] = jnp.zeros_like(bias_grad_ref)

    @pl.when(active == windows)
    def _():
        prepare()
        total = None
        for i in range(windows):
            lanes = slice(i * span, (i + 1) * span)
            logits = jnp.dot(weight_ref[...], columns_ref[:, lanes], preferred_element_type=F32)
            part, low = slopes(logits, i)
            total = part if total is None else total + part
            grads_ref[:, lanes] = low
        bias_grad_ref[...] = jnp.sum(total.T, axis=0, keepdims=True)
        product = jnp.dot(grads_ref[...], rows_ref[...], preferred_element_type=F32)
        store(product.astype(BF16))

    @pl.when((active > 0) & (active < windows))
    def _():
        prepare()
        grads_ref[...] = jnp.zeros_like(grads_ref)
        sums_ref[...] = jnp.zeros_like(sums_ref)
        total_ref[...] = jnp.zeros_like(total_ref)

        def one(window):
            at = window * span
            lanes = pl.ds(at if isinstance(window, int) else pl.multiple_of(at, span), span)
            logits = jnp.dot(weight_ref[...], columns_ref[:, lanes], preferred_element_type=F32)
            part, low = slopes(logits, window)
            sums_ref[...] += part
            grads_ref[:, lanes] = low
            total_ref[...] += jnp.dot(low, rows_ref[lanes, :], preferred_element_type=F32)
            return 0

        if span % LANES == 0:
            lax.fori_loop(0, active, lambda i, _: one(windows_ref[skipped + i]), 0)
        else:
            for i in range(windows):

                @pl.when((species_ref[i] == 1) == is_mouse)
                def _():
                    one(i)
        bias_grad_ref[...] = jnp.sum(sums_ref[...].T, axis=0, keepdims=True)
        store(total_ref[...].astype(BF16))


def head(
    species, order, humans, core, mouse, human, bias_mouse, bias_human, counts, rows, columns, scales,
    mouse_tiles, first_human, human_tiles, split,
):
    tokens, width = rows.shape
    lane = counts.shape[1]
    tracks = (human.shape[0], mouse.shape[0])
    tiles = mouse_tiles + human_tiles
    at_mouse = lambda j: jnp.minimum(j, max(mouse_tiles - 1, 0))
    at_human = lambda j: first_human + jnp.maximum(j - mouse_tiles, 0)
    at_both = lambda j: jnp.where(j < mouse_tiles, j, first_human + j - mouse_tiles)
    fixed = lambda j, *_: (0, 0)
    out = lambda j, *_: (j, 0)
    strip = width // 2 if split else width
    copies = 2 if split else 1
    return pl.pallas_call(
        functools.partial(
            head_body, mouse_tiles=mouse_tiles, first_human=first_human, tracks=tracks, scales=scales
        ),
        grid_spec=pltpu.PrefetchScalarGridSpec(
            num_scalar_prefetch=4,
            grid=(tiles,),
            in_specs=[
                pl.BlockSpec((TILE, width), lambda j, *_: (at_mouse(j), 0)),
                pl.BlockSpec((TILE, width), lambda j, *_: (at_human(j), 0)),
                pl.BlockSpec((1, TILE), lambda j, *_: (0, at_mouse(j))),
                pl.BlockSpec((1, TILE), lambda j, *_: (0, at_human(j))),
                pl.BlockSpec((TILE * tokens // lane, lane), lambda j, *_: (at_both(j), 0)),
                pl.BlockSpec((tokens, width), fixed),
                pl.BlockSpec((width, tokens), fixed),
            ],
            out_specs=[pl.BlockSpec((TILE, strip), out)] * copies
            + [pl.BlockSpec((TILE, tokens), out), pl.BlockSpec((1, TILE), lambda j, *_: (0, j))],
            scratch_shapes=[
                pltpu.VMEM((TILE, width), BF16),
                pltpu.VMEM((TILE, LANES), F32),
                pltpu.VMEM((TILE, lane), F32),
                pltpu.VMEM((TILE, width), F32),
            ],
        ),
        out_shape=[jax.ShapeDtypeStruct((tiles * TILE, strip), BF16)] * copies
        + [
            jax.ShapeDtypeStruct((tiles * TILE, tokens), BF16),
            jax.ShapeDtypeStruct((1, tiles * TILE), F32),
        ],
        compiler_params=pltpu.CompilerParams(vmem_limit_bytes=58 * 2**20),
        cost_estimate=pl.CostEstimate(
            flops=4 * tiles * TILE * width * tokens,
            bytes_accessed=tiles * TILE * (tokens * 6 + width * 4),
            transcendentals=3 * tiles * TILE * tokens,
        ),
    )(species, order, humans, core, mouse, human, bias_mouse, bias_human, counts, rows, columns)


def back_body(
    humans_ref, mouse_ref, human_ref, early_ref, late_ref, out_ref, total_ref,
    *, mouse_tiles, early_tiles, tracks, windows,
):
    step = pl.program_id(0)
    tile = mouse_ref.shape[0]
    is_mouse = step < mouse_tiles
    row = lax.broadcasted_iota(jnp.int32, (tile, 1), 0)

    @pl.when(step == 0)
    def _():
        total_ref[...] = jnp.zeros_like(total_ref)

    @pl.when(is_mouse & (humans_ref[0] < windows))
    def _():
        inside = step * tile + row < tracks[1]
        weight = jnp.where(inside, mouse_ref[...], BF16(0)).T
        total_ref[...] += jnp.dot(weight, early_ref[...], preferred_element_type=F32)

    def human(grads_ref):
        inside = (step - mouse_tiles) * tile + row < tracks[0]
        weight = jnp.where(inside, human_ref[...], BF16(0)).T
        total_ref[...] += jnp.dot(weight, grads_ref[...], preferred_element_type=F32)

    some = humans_ref[0] > 0

    @pl.when((step >= mouse_tiles) & (step < early_tiles) & some)
    def _():
        human(early_ref)

    @pl.when((step >= early_tiles) & some)
    def _():
        human(late_ref)

    @pl.when(step == pl.num_programs(0) - 1)
    def _():
        out_ref[...] = total_ref[...].T


def head_back(humans, windows, mouse, human, early, late):
    tokens = early.shape[1]
    width = human.shape[1]
    mouse_tiles = pl.cdiv(mouse.shape[0], TILE)
    early_tiles = early.shape[0] // TILE
    tiles = early_tiles + late.shape[0] // TILE
    return pl.pallas_call(
        functools.partial(
            back_body,
            mouse_tiles=mouse_tiles,
            early_tiles=early_tiles,
            tracks=(human.shape[0], mouse.shape[0]),
            windows=windows,
        ),
        grid_spec=pltpu.PrefetchScalarGridSpec(
            num_scalar_prefetch=1,
            grid=(tiles,),
            in_specs=[
                pl.BlockSpec((TILE, width), lambda j, *_: (jnp.minimum(j, mouse_tiles - 1), 0)),
                pl.BlockSpec((TILE, width), lambda j, *_: (jnp.maximum(j - mouse_tiles, 0), 0)),
                pl.BlockSpec((TILE, tokens), lambda j, *_: (jnp.minimum(j, early_tiles - 1), 0)),
                pl.BlockSpec((TILE, tokens), lambda j, *_: (jnp.maximum(j - early_tiles, 0), 0)),
            ],
            out_specs=pl.BlockSpec((tokens, width), lambda j, *_: (0, 0)),
            scratch_shapes=[pltpu.VMEM((width, tokens), F32)],
        ),
        out_shape=jax.ShapeDtypeStruct((tokens, width), F32),
        compiler_params=pltpu.CompilerParams(vmem_limit_bytes=58 * 2**20),
        cost_estimate=pl.CostEstimate(
            flops=2 * tiles * TILE * width * tokens,
            bytes_accessed=tiles * TILE * (tokens + width) * 2,
            transcendentals=0,
        ),
    )(humans, mouse, human, early, late)


def widen_body(in_ref, out_ref):
    out_ref[...] = in_ref[0].astype(F32)


def widen_head(tracks, summed, before, early):
    devices, rows, width = summed.shape
    block = rows // 2
    place = lambda j: (jnp.where(j < early, before + j, j - early), jnp.where(j < early, 0, 1), 0)
    return pl.pallas_call(
        widen_body,
        grid=(pl.cdiv(tracks, block),),
        in_specs=[pl.BlockSpec((1, block, width), place)],
        out_specs=pl.BlockSpec((block, width), lambda j: (j, 0)),
        out_shape=jax.ShapeDtypeStruct((tracks, width), F32),
        compiler_params=pltpu.CompilerParams(vmem_limit_bytes=60 * 2**20),
    )(summed)


def weights_body(core_ref, mine_ref, other_ref, conv_ref, proj_ref, sums_ref):
    half, middle = mine_ref.shape
    taken = conv_ref.shape[0]
    strips = proj_ref.shape[1] // middle

    def spread(first, second):
        def rows(start, count):
            parts = []
            if start < half:
                parts.append(first[start : min(half, start + count), :])
            if start + count > half:
                parts.append(second[max(0, start - half) : start + count - half, :])
            parts = [part.astype(F32) for part in parts]
            return parts[0] if len(parts) == 1 else jnp.concatenate(parts, axis=0)

        conv_ref[...] = rows(0, taken)
        for i in range(strips):
            proj_ref[:, i * middle : (i + 1) * middle] = rows(
                taken + i * proj_ref.shape[0], proj_ref.shape[0]
            )
        sums_ref[...] = rows(taken + strips * proj_ref.shape[0], sums_ref.shape[0])

    @pl.when(core_ref[0] == 0)
    def _():
        spread(mine_ref, other_ref)

    @pl.when(core_ref[0] != 0)
    def _():
        spread(other_ref, mine_ref)


def finish_weights(core, mine, other, taken, proj_shape):
    half, middle = mine.shape
    rest = 2 * half - taken - proj_shape[0] * proj_shape[1] // middle
    shapes = [(taken, middle), proj_shape, (rest, middle)]
    whole = lambda shape: pl.BlockSpec(shape, lambda j, *_: (0, 0))
    return pl.pallas_call(
        weights_body,
        grid_spec=pltpu.PrefetchScalarGridSpec(
            num_scalar_prefetch=1,
            grid=(1,),
            in_specs=[whole((half, middle))] * 2,
            out_specs=[whole(shape) for shape in shapes],
        ),
        out_shape=[jax.ShapeDtypeStruct(shape, F32) for shape in shapes],
        compiler_params=pltpu.CompilerParams(vmem_limit_bytes=60 * 2**20),
    )(core, mine, other)


def on_device(
    block_in,
    gain_in,
    shift_in,
    dilated_taps_weight,
    gain_mid,
    shift_mid,
    proj_weight,
    proj_bias,
    head_human,
    bias_human,
    head_mouse,
    bias_mouse,
    species,
    counts,
):
    windows, span, width = block_in.shape
    tokens = windows * span
    middle = proj_weight.shape[0]
    tracks_human = head_human.shape[1]
    tracks_mouse = head_mouse.shape[1]
    devices = lax.axis_size(EVERY)
    population = float(tokens * devices)
    core = lax.axis_index("core").astype(jnp.int32)[None]

    wide = block_in.reshape(tokens, width).astype(F32)
    sent, finish = small_sum([jnp.sum(wide, axis=0), jnp.sum(wide * wide, axis=0)])
    before, after = [move(value) for value, move in edges(block_in, DILATION_STEP)]
    everyone = to_all(sent)
    sum_in, square_in = finish(everyone)
    centre_in, scale_in = statistics(sum_in, square_in, population)

    def activate_in(values):
        return gelu_pair((values.astype(F32) - centre_in) * scale_in * gain_in + shift_in)

    normed_in = (wide - centre_in) * scale_in
    hidden_in, slope_in = gelu_pair(normed_in * gain_in + shift_in)
    hidden_in = hidden_in.astype(BF16).reshape(windows, span, width)
    place = lax.axis_index(BINS)
    last = lax.axis_size(BINS) - 1
    hidden_before = jnp.where(place > 0, activate_in(before)[0], 0.0).astype(BF16)
    hidden_after = jnp.where(place < last, activate_in(after)[0], 0.0).astype(BF16)
    padded = jnp.concatenate([hidden_before, hidden_in, hidden_after], axis=1)
    shifted = taps(padded, span)
    dilated = sum(
        jnp.dot(rows, dilated_taps_weight[k], preferred_element_type=F32)
        for k, rows in enumerate(shifted)
    )
    sent, finish = small_sum([jnp.sum(dilated, axis=0), jnp.sum(dilated * dilated, axis=0)])
    sum_mid, square_mid = finish(to_all(sent))
    centre_mid, scale_mid = statistics(sum_mid, square_mid, population)
    normed_mid = (dilated - centre_mid) * scale_mid
    hidden_mid, slope_mid = gelu_pair(normed_mid * gain_mid + shift_mid)
    hidden_mid = hidden_mid.astype(BF16)
    branch = jnp.dot(hidden_mid, proj_weight, preferred_element_type=F32)
    block_out = (wide + branch + proj_bias).astype(BF16)

    lane = min(span, LANES)
    counts_rows = (
        counts.transpose(2, 0, 1)
        .reshape(tracks_human, windows, span // lane, lane)
        .transpose(0, 2, 1, 3)
        .reshape(-1, lane)
    )
    columns = block_out.T
    scales = (math.sqrt(width / tracks_human), math.sqrt(width / tracks_mouse))
    by_species = jnp.argsort(species).astype(jnp.int32)
    humans = jnp.sum(species == 0).astype(jnp.int32)[None]
    mouse_tiles, human_tiles = pl.cdiv(tracks_mouse, TILE), pl.cdiv(tracks_human, TILE)
    early_tiles = (mouse_tiles + human_tiles) // 2 - mouse_tiles
    late_tiles = human_tiles - early_tiles
    mouse, human = head_mouse.T, head_human.T

    def some_tiles(*which):
        return head(
            species, by_species, humans, core, mouse, human, bias_mouse[None], bias_human[None],
            counts_rows, block_out, columns, scales, *which,
        )

    scatter = lambda value, axes: lax.psum_scatter(value, axes, scatter_dimension=0, tiled=True)
    gather = lambda value, axes: lax.all_gather(value, axes, axis=0, tiled=True)
    across, along, deep = bits_of("x"), bits_of("y"), bits_of("batch")
    order = Order()
    early, slopes_early, bias_early = some_tiles(mouse_tiles, 0, early_tiles, False)
    order.token = [bias_early]
    early = scatter(early, BINS)
    late, slopes_late, bias_late = order.run(
        lambda *_: some_tiles(0, early_tiles, late_tiles, False), bias_early
    )
    order.token = [bias_late]
    late = scatter(late, BINS)
    output_grad = order.run(
        lambda early, late: head_back(humans, windows, mouse, human, early, late),
        slopes_early,
        slopes_late,
    )
    to_core = lambda value: swap(value, CORE)
    chips = lax.axis_size(CHIPS)
    unit = 16 * chips

    def cut(rows, count):
        count = min(count, rows // unit)
        ends = [rows // unit * (i + 1) // count * unit for i in range(count)]
        return [end - start for end, start in zip(ends, [0] + ends[:-1])]

    def after_head(output_grad):
        branch_grad = output_grad.astype(BF16)
        mid_grad = back_product(branch_grad, proj_weight) * slope_mid
        sent, _ = small_sum([jnp.sum(mid_grad, axis=0), jnp.sum(mid_grad * normed_mid, axis=0)])
        return sent, branch_grad, mid_grad

    sent, branch_grad, mid_grad = order.run(after_head, output_grad)
    everyone = to_all(sent)

    def weight_work(branch_grad, output_grad):
        product = rows_product(hidden_mid, branch_grad).reshape(middle, width // middle, middle)
        return product.swapaxes(0, 1).reshape(-1, middle), jnp.sum(output_grad, axis=0)

    proj_grad, proj_bias_grad = order.run(weight_work, branch_grad, output_grad)

    def middle_work(everyone, mid_grad):
        _, finish = small_sum([shift_mid, gain_mid])
        shift_mid_grad, gain_mid_grad = finish(everyone)
        dilated_grad = scale_mid * gain_mid * (
            mid_grad - shift_mid_grad / population - normed_mid * gain_mid_grad / population
        )
        return dilated_grad.astype(BF16), shift_mid_grad, gain_mid_grad

    dilated_grad, shift_mid_grad, gain_mid_grad = order.run(middle_work, everyone, mid_grad)
    dilated_windows = dilated_grad.reshape(windows, span, middle)
    grad_before, grad_after = [move(value) for value, move in edges(dilated_windows, DILATION_STEP)]
    sums = jnp.concatenate(
        [
            proj_bias_grad,
            bias_early[0, mouse_tiles * TILE :],
            bias_late[0, : tracks_human - early_tiles * TILE],
            bias_early[0, :tracks_mouse],
        ]
    )
    weight_rows = pl.cdiv(4 * width * middle + sums.size, middle)
    all_rows = pl.cdiv(weight_rows, 4 * unit) * 4 * unit
    half = all_rows // 2

    def conv_work(dilated_grad, proj_grad, sums):
        parts = [rows_product(rows, dilated_grad) for rows in shifted] + [proj_grad]
        fill = (all_rows - 4 * width) * middle - sums.size
        parts.append(jnp.pad(sums, (0, fill)).reshape(-1, middle))
        grads = jnp.concatenate(parts, axis=0)
        return lax.dynamic_slice_in_dim(grads, (1 - core[0]) * half, half, 0), grads

    weights_send, weights_grad = order.run(conv_work, dilated_grad, proj_grad, sums)
    weights_arrived = to_core(weights_send)
    weights_keep = lax.dynamic_slice_in_dim(weights_grad, core[0] * half, half, 0)
    weights = Group(
        order,
        [weights_keep, weights_arrived],
        cut(half, 2),
        0,
        (across + along + deep, along + across + deep),
    )
    weights.step()

    def hidden_work(grad_before, dilated_windows, grad_after):
        grad_shifted = taps(
            jnp.concatenate([grad_before, dilated_windows, grad_after], axis=1), span
        )
        hidden_grad = sum(
            back_product(grad_shifted[2 - k], dilated_taps_weight[k]) for k in range(3)
        )
        in_grad = hidden_grad * slope_in
        sent, _ = small_sum([jnp.sum(in_grad, axis=0), jnp.sum(in_grad * normed_in, axis=0)])
        return sent, in_grad

    sent, in_grad = order.run(hidden_work, grad_before, dilated_windows, grad_after)
    everyone = to_all(sent)
    weights.step()

    def last_work(everyone, output_grad, in_grad):
        _, finish = small_sum([shift_in, gain_in])
        shift_in_grad, gain_in_grad = finish(everyone)
        input_grad = output_grad + scale_in * gain_in * (
            in_grad - shift_in_grad / population - normed_in * gain_in_grad / population
        )
        return input_grad.astype(BF16), shift_in_grad, gain_in_grad

    input_grad, shift_in_grad, gain_in_grad = order.run(last_work, everyone, output_grad, in_grad)
    weights.step()
    summed = order.run(lambda *both: jnp.concatenate(both, axis=0), early, late)
    summed = scatter(summed, "batch")
    weights.step()
    weights.step()
    summed = gather(order.run(lambda value: value, summed), "batch")
    weights.step()
    weights.step()
    summed = gather(order.run(lambda value: value, summed), BINS)
    while not weights.done():
        weights.step()
    summed = summed.reshape(lax.axis_size(BINS), -1, width)
    weights_mine = weights.shares[0]
    weights_other = to_core(weights_mine)
    conv_total, proj_total, sums_total = order.run(
        lambda mine, other: finish_weights(core, mine, other, 3 * width, (middle, width)),
        weights_mine,
        weights_other,
    )
    conv_total = conv_total.reshape(3, width, middle)
    conv_total = conv_total.reshape(3, width, middle)
    sums_total = sums_total.reshape(-1)
    ends = [0, width, width + tracks_human, width + tracks_human + tracks_mouse]
    proj_bias_total, bias_human_grad, bias_mouse_grad = [
        sums_total[low:high] for low, high in zip(ends[:-1], ends[1:])
    ]
    per_tile = TILE // (summed.shape[1] // 2)
    mouse_blocks, early_blocks = mouse_tiles * per_tile, early_tiles * per_tile
    head_mouse_grad = widen_head(tracks_mouse, summed, 0, mouse_blocks)
    head_human_grad = widen_head(tracks_human, summed, mouse_blocks, early_blocks)
    return (
        block_out.reshape(windows, span, width),
        input_grad.reshape(windows, span, width),
        gain_in_grad,
        shift_in_grad,
        conv_total,
        gain_mid_grad,
        shift_mid_grad,
        proj_total,
        proj_bias_total,
        head_human_grad.T,
        bias_human_grad,
        head_mouse_grad.T,
        bias_mouse_grad,
    )


def solution(mesh):
    bins, batch = mesh.shape["bins"], mesh.shape["batch"]
    side = 1 << (((bins // 2).bit_length() - 1) // 2)
    grid = jax.sharding.Mesh(
        mesh.devices.reshape(bins // 2 // side, side, 2, batch), ("y", "x", "core", "batch")
    )
    tokens = P("batch", BINS, None)
    placed = (tokens,) + (P(),) * 11 + (P("batch"), tokens)
    return jax.shard_map(
        on_device,
        mesh=grid,
        in_specs=placed,
        out_specs=(tokens, tokens) + (P(),) * 11,
        check_vma=False,
    )
```

time: 486 us -> 445 us (0.916)
  other arithmetic: 77.2 us -> 27.7 us
  starting transfers between devices: 88.3 us -> 44.1 us
  Pallas kernels: 104 us -> 140 us
  blocking collectives: 14.1 us -> 0 us
  between operations: 2.33 us -> 14.9 us
  local copies, waits for them, and re-layouts: 23.4 us -> 35.1 us
  waiting for transfers between devices: 146 us -> 152 us
    ppermute x53 -> x18, waiting for transfers between devices: 128 us -> 83.6 us  [swap(): return lax.ppermute(value, axis, [(i, i ^ mask) for i in range(size)])]
    pallas_call x6 -> x15, Pallas kernels: 104 us -> 140 us  [the longest x2 68.1 us: head(): pl.pallas_call(functools.partial(head_body, mouse_tiles=mouse_tiles, firs...]
    ppermute x53 -> x18, starting transfers between devices: 54.4 us -> 19.4 us  [swap(): return lax.ppermute(value, axis, [(i, i ^ mask) for i in range(size)])]
    convert_element_type x27 -> x2, other arithmetic: 39.1 us -> 7.23 us  [the longest x1 4.54 us: last_work(): return (input_grad.astype(BF16), shift_in_grad, gain_in_grad)]
    all_gather x0 -> x2, waiting for transfers between devices: none -> 29.6 us  [on_device(): gather = lambda value, axes: lax.all_gather(value, axes, axis=0, tiled=True)]
    all_to_all x5 -> x4, waiting for transfers between devices: 17.6 us -> 38.4 us  [to_all(): return lax.all_to_all(sent, axes, 0, 0, tiled=True)]
    all_to_all x1 -> x0, blocking collectives: 14.1 us -> none  [to_all(): return lax.all_to_all(sent, axes, 0, 0, tiled=True)]
    all_to_all x5 -> x4, starting transfers between devices: 27.1 us -> 15.5 us  [to_all(): return lax.all_to_all(sent, axes, 0, 0, tiled=True)]
  transfers between devices with their start and end apart: 62 -> 31, of which waited for: 21 -> 20; matrix products, arithmetic and copies ran while one was open for 8% -> 13% of each run, Pallas kernels for 16% -> 20%
where the time goes in v1:
time: 445 us; the launch traced here: 438 us
  waiting for transfers between devices  152 us (34%)
  Pallas kernels  140 us (31%)
  starting transfers between devices  44.1 us (10%)
  local copies, waits for them, and re-layouts  35.1 us (8%)
  other arithmetic  27.7 us (6%)
  matrix products  24 us (5%)
  between operations  14.9 us (3%)
    ppermute x18, waiting for transfers between devices, swap(): return lax.ppermute(value, axis, [(i, i ^ mask) for i in range(size)])  83.6 us
    pallas_call x2, Pallas kernels, head(): pl.pallas_call(functools.partial(head_body, mouse_tiles=mouse_tiles, firs...  68.1 us
    all_to_all x4, waiting for transfers between devices, to_all(): return lax.all_to_all(sent, axes, 0, 0, tiled=True)  38.4 us
    all_gather x2, waiting for transfers between devices, on_device(): gather = lambda value, axes: lax.all_gather(value, axes, axis=0, tiled=True)  29.6 us
    pallas_call x1, Pallas kernels, head_back(): pl.pallas_call(functools.partial(back_body, mouse_tiles=mouse_tiles, earl...  22.1 us
    ppermute x18, starting transfers between devices, swap(): return lax.ppermute(value, axis, [(i, i ^ mask) for i in range(size)])  19.4 us
    pallas_call x2, Pallas kernels, widen_head(): pl.pallas_call(widen_body, grid=(pl.cdiv(tracks, block),), in_specs=[pl.B...  16.4 us
    pallas_call x5, Pallas kernels, sum_parts(): pl.pallas_call(functools.partial(sum_body, counts=counts), grid_spec=pltp...  15.9 us
  transfers between devices with their start and end apart: 31, of which 20 were waited for; matrix products, arithmetic and copies ran while one was open for 13% of the time, Pallas kernels for 20%

profile of v1, /device:TPU:0, one launch (start us, length us, event | category | flops | bytes accessed | tf_op | source)
XLA Modules:
  0.0 437.5 jit_solution(8726561668164000553)
XLA Ops:
  10.0 7.3 %all-to-all-start = ((f32[32,1,1536]{2,1,0:T(1,128)}), f32[32,1,1536]{2,1,0:T(1,128)S(1)}, u32[]{:S(2)}, u32[]{:S(2)}) async-start(f32[32,1,1536]{2,1,0:T(1,128)} %broadcast_in_dim.21), calls=%async_computation | async-start | bytes 393216 | tf_op jit(solution)/shard_map/all_to_all | solution.py:45
  21.7 4.9 %all-to-all-done = f32[32,1,1536]{2,1,0:T(1,128)S(1)} async-done(((f32[32,1,1536]{2,1,0:T(1,128)}), f32[32,1,1536]{2,1,0:T(1,128)S(1)}, u32[]{:S(2)}, u32[]{:S(2)}) %all-to-all-start) | async-done | bytes 196640 | tf_op jit(solution)/shard_map/all_to_all | solution.py:45
  40.5 5.3 %all-to-all-done.1 = f32[32,1,768]{2,1,0:T(1,128)S(1)} async-done(((f32[32,1,768]{2,1,0:T(1,128)}), f32[32,1,768]{2,1,0:T(1,128)S(1)}, u32[]{:S(2)}, u32[]{:S(2)}) %all-to-all-start.1) | async-done | bytes 98336 | tf_op jit(solution)/shard_map/all_to_all | solution.py:45
  52.9 37.7 %shard_map.238 = (bf16[3584,768]{1,0:T(8,128)(2,1)}, bf16[3584,1024]{1,0:T(8,128)(2,1)}, f32[1,3584]{1,0:T(1,128)}) custom-call(s32[4]{0:T(128)} %species_ref.3, s32[4]{0:T(128)} %get-tuple-element.109.windows_ref, s32[1]{0:T(128)} %bitcast.8.humans_ref, s32[1]{0:T(128)} %bitcast.11.core_ref, bf16[1643,768]{1,0:T(8,128)(2,1)} %bitcast.169, ...), custom_call_target="tpu_custom_call" | custom-call | flops 11274289152 | bytes 33030144 | tf_op jit(solution)/shard_map/pallas_call | solution.py:397
  93.0 30.4 %shard_map.237 = (bf16[3584,768]{1,0:T(8,128)(2,1)}, bf16[3584,1024]{1,0:T(8,128)(2,1)}, f32[1,3584]{1,0:T(1,128)}) custom-call(s32[4]{0:T(128)} %species_ref.3, s32[4]{0:T(128)} %get-tuple-element.109.windows_ref, s32[1]{0:T(128)} %bitcast.8.humans_ref, s32[1]{0:T(128)} %bitcast.11.core_ref, bf16[1643,768]{1,0:T(8,128)(2,1)} %bitcast.170, ...), custom_call_target="tpu_custom_call" | custom-call | flops 11274289152 | bytes 33030144 | tf_op jit(solution)/shard_map/pallas_call | solution.py:397
  123.3 22.1 %shard_map.239 = f32[1024,768]{1,0:T(8,128)} custom-call(s32[1]{0:T(128)} %bitcast.8.humans_ref, bf16[1643,768]{1,0:T(8,128)(2,1)} %bitcast.171, bf16[5313,768]{1,0:T(8,128)(2,1)} %bitcast.167, bf16[3584,1024]{1,0:T(8,128)(2,1)} %get-tuple-element.113.early_ref, bf16[3584,1024]{1,0:T(8,128)(2,1)} %get-tuple-element.114.late_ref), custom_call_target="tpu_custom_call" | custom-call | flops 11274289152 | bytes 25690112 | tf_op jit(solution)/shard_map/pallas_call | solution.py:481
  162.2 7.0 %all-to-all-done.2 = f32[32,1,768]{2,1,0:T(1,128)S(1)} async-done(((f32[32,1,768]{2,1,0:T(1,128)}), f32[32,1,768]{2,1,0:T(1,128)S(1)}, u32[]{:S(2)}, u32[]{:S(2)}) %all-to-all-start.2) | async-done | bytes 98336 | tf_op jit(solution)/shard_map/all_to_all | solution.py:45
  200.7 4.0 fusion.50
  210.0 21.1 %all-to-all-done.3 = f32[32,1,1536]{2,1,0:T(1,128)S(1)} async-done(((f32[32,1,1536]{2,1,0:T(1,128)}), f32[32,1,1536]{2,1,0:T(1,128)S(1)}, u32[]{:S(2)}, u32[]{:S(2)}) %all-to-all-start.3) | async-done | bytes 196640 | tf_op jit(solution)/shard_map/all_to_all | solution.py:45
  238.9 4.5 %fusion.26 = bf16[1024,768]{1,0:T(8,128)(2,1)} fusion(f32[1024,768]{1,0:T(8,128)S(1)} %copy-done.3, bf16[4,256,768]{2,1,0:T(8,128)(2,1)} %param.14, f32[1024,768]{1,0:T(8,128)} %get-tuple-element.141, f32[768]{0:T(1024)S(1)} %get-tuple-element.232, f32[768]{0:T(1024)S(1)} %get-tuple-element.213, f32[768]{0:T(1024)} %get-tuple-element.229, ...), kind=kLoop, calls=%fused_computation.31 | loop fusion | flops 7864320 | bytes 9452544 | tf_op jit(solution)/shard_map/convert_element_type | solution.py:761
  243.4 9.1 %collective-permute-done.8.refs_7_.refs_8_.refs_9_ = f32[256,384]{1,0:T(8,128)S(1)} collective-permute-done((f32[256,384]{1,0:T(8,128)}, f32[256,384]{1,0:T(8,128)S(1)}, u32[]{:S(2)}, u32[]{:S(2)}) %collective-permute-start.8) | collective-permute-done | bytes 393248 | tf_op jit(solution)/shard_map/ppermute | solution.py:51
  261.4 5.1 %collective-permute-done.10.refs_9_.refs_10_ = f32[128,384]{1,0:T(8,128)S(1)} collective-permute-done((f32[128,384]{1,0:T(8,128)S(1)}, f32[128,384]{1,0:T(8,128)S(1)}, u32[]{:S(2)}, u32[]{:S(2)}) %collective-permute-start.10) | collective-permute-done | bytes 196640 | tf_op jit(solution)/shard_map/ppermute | solution.py:51
  266.6 8.6 %collective-permute-done.9.refs_4_ = f32[128,384]{1,0:T(8,128)S(1)} collective-permute-done((f32[128,384]{1,0:T(8,128)S(1)}, f32[128,384]{1,0:T(8,128)S(1)}, u32[]{:S(2)}, u32[]{:S(2)}) %collective-permute-start.9) | collective-permute-done | bytes 196640 | tf_op jit(solution)/shard_map/ppermute | solution.py:51
  278.6 4.2 collective-permute-start.12
  283.4 12.4 %collective-permute-done.12.refs_11_ = f32[64,384]{1,0:T(8,128)S(1)} collective-permute-done((f32[64,384]{1,0:T(8,128)}, f32[64,384]{1,0:T(8,128)S(1)}, u32[]{:S(2)}, u32[]{:S(2)}) %collective-permute-start.12) | collective-permute-done | bytes 98336 | tf_op jit(solution)/shard_map/ppermute | solution.py:51
  295.8 4.1 collective-permute-done.11.refs_5_
  315.4 8.3 %collective-permute-done.16.refs_3_ = bf16[128,384]{1,0:T(8,128)(2,1)S(1)} collective-permute-done((bf16[128,384]{1,0:T(8,128)(2,1)}, bf16[128,384]{1,0:T(8,128)(2,1)S(1)}, u32[]{:S(2)}, u32[]{:S(2)}) %collective-permute-start.16) | collective-permute-done | bytes 98336 | tf_op jit(solution)/shard_map/ppermute | solution.py:51
  323.7 5.7 %collective-permute-done.15.refs_1_ = bf16[128,384]{1,0:T(8,128)(2,1)S(1)} collective-permute-done((bf16[128,384]{1,0:T(8,128)(2,1)}, bf16[128,384]{1,0:T(8,128)(2,1)S(1)}, u32[]{:S(2)}, u32[]{:S(2)}) %collective-permute-start.15) | collective-permute-done | bytes 98336 | tf_op jit(solution)/shard_map/ppermute | solution.py:51
  332.5 6.1 %all-gather.3.cloned.1.call-done = bf16[896,768]{1,0:T(8,128)(2,1)} async-done(((bf16[224,768]{1,0:T(8,128)(2,1)}), bf16[896,768]{1,0:T(8,128)(2,1)}) %all-gather.3.cloned.1.call-update) | async-done | bytes 1376272 | tf_op jit(solution)/shard_map/all_gather | solution.py:658
  352.5 18.0 %collective-permute-done.20.refs_3_ = bf16[512,384]{1,0:T(8,128)(2,1)S(1)} collective-permute-done((bf16[512,384]{1,0:T(8,128)(2,1)}, bf16[512,384]{1,0:T(8,128)(2,1)S(1)}, u32[]{:S(2)}, u32[]{:S(2)}) %collective-permute-start.20) | collective-permute-done | bytes 393248 | tf_op jit(solution)/shard_map/ppermute | solution.py:51
  380.7 6.0 %shard_map.249 = (f32[2304,384]{1,0:T(8,128)}, f32[384,768]{1,0:T(8,128)}, f32[1024,384]{1,0:T(8,128)}) custom-call(s32[1]{0:T(128)} %bitcast.11.core_ref, bf16[2048,384]{1,0:T(8,128)(2,1)} %shard_map.248.mine_ref, bf16[2048,384]{1,0:T(8,128)(2,1)} %copy-done.19), custom_call_target="tpu_custom_call" | custom-call | tf_op jit(solution)/shard_map/pallas_call | solution.py:565
  390.7 23.5 %all-gather.5.cloned.1.call-done = bf16[7168,768]{1,0:T(8,128)(2,1)} async-done(((bf16[896,768]{1,0:T(8,128)(2,1)}), bf16[7168,768]{1,0:T(8,128)(2,1)}) %all-gather.5.cloned.1.call-update) | async-done | bytes 11010064 | tf_op jit(solution)/shard_map/all_gather | solution.py:658
  414.2 4.5 %shard_map.251 = f32[1643,768]{1,0:T(8,128)} custom-call(bf16[8,896,768]{2,1,0:T(8,128)(2,1)} %bitcast.143), custom_call_target="tpu_custom_call" | custom-call | tf_op jit(solution)/shard_map/pallas_call | solution.py:519
  418.7 11.8 %shard_map.250 = f32[5313,768]{1,0:T(8,128)} custom-call(bf16[8,896,768]{2,1,0:T(8,128)(2,1)} %bitcast.144), custom_call_target="tpu_custom_call" | custom-call | tf_op jit(solution)/shard_map/pallas_call | solution.py:519
  (227 shorter events, 150.6 us)
Async XLA Ops:
  10.0 16.6 %all-to-all-start = ((f32[32,1,1536]{2,1,0:T(1,128)}), f32[32,1,1536]{2,1,0:T(1,128)S(1)}, u32[]{:S(2)}, u32[]{:S(2)}) async-start(f32[32,1,1536]{2,1,0:T(1,128)} %broadcast_in_dim.21), calls=%async_computation | async-start | bytes 393216 | tf_op jit(solution)/shard_map/all_to_all | solution.py:45
  17.4 12.5 %collective-permute-start.1 = (bf16[4,11,768]{2,1,0:T(8,128)(2,1)S(1)}, bf16[4,11,768]{2,1,0:T(8,128)(2,1)S(1)}, u32[]{:S(2)}, u32[]{:S(2)}) collective-permute-start(bf16[4,11,768]{2,1,0:T(8,128)(2,1)S(1)} %get-tuple-element.221), channel_id=1, source_target_pairs={{4,0},{8,4},{12,8},{16,12},{20,16},{24,20},{28,24},{5,1},{9,5},{13... | collective-permute-start | bytes 202760 | tf_op jit(solution)/shard_map/ppermute | solution.py:249
  18.7 11.2 %collective-permute-start = (bf16[4,11,768]{2,1,0:T(8,128)(2,1)S(1)}, bf16[4,11,768]{2,1,0:T(8,128)(2,1)S(1)}, u32[]{:S(2)}, u32[]{:S(2)}) collective-permute-start(bf16[4,11,768]{2,1,0:T(8,128)(2,1)S(1)} %get-tuple-element.222), channel_id=1, source_target_pairs={{0,4},{4,8},{8,12},{12,16},{16,20},{20,24},{24,28},{1,5},{5,9},{9,... | collective-permute-start | bytes 202760 | tf_op jit(solution)/shard_map/ppermute | solution.py:248
  35.3 10.5 %all-to-all-start.1 = ((f32[32,1,768]{2,1,0:T(1,128)}), f32[32,1,768]{2,1,0:T(1,128)S(1)}, u32[]{:S(2)}, u32[]{:S(2)}) async-start(f32[32,1,768]{2,1,0:T(1,128)} %broadcast_in_dim.23), calls=%async_computation.1 | async-start | bytes 196608 | tf_op jit(solution)/shard_map/all_to_all | solution.py:45
  37.9 218.3 %reduce-scatter.6.cloned.1.call-start = ((), (), s32[]{:S(2)}) async-start(), calls=%async_computation.8 | async-start | bytes 6193152 | tf_op jit(solution)/shard_map/reduce_scatter | solution.py:657
  158.7 10.5 %all-to-all-start.2 = ((f32[32,1,768]{2,1,0:T(1,128)}), f32[32,1,768]{2,1,0:T(1,128)S(1)}, u32[]{:S(2)}, u32[]{:S(2)}) async-start(f32[32,1,768]{2,1,0:T(1,128)} %broadcast_in_dim.28), calls=%async_computation.2 | async-start | bytes 196608 | tf_op jit(solution)/shard_map/all_to_all | solution.py:45
  161.3 94.9 %reduce-scatter.4.cloned.1.call-start = ((), (), s32[]{:S(2)}) async-start(), calls=%async_computation.7 | async-start | bytes 6193152 | tf_op jit(solution)/shard_map/reduce_scatter | solution.py:657
  183.0 12.2 %collective-permute-start.3 = (bf16[4,11,384]{2,1,0:T(8,128)(2,1)S(1)}, bf16[4,11,384]{2,1,0:T(8,128)(2,1)S(1)}, u32[]{:S(2)}, u32[]{:S(2)}) collective-permute-start(bf16[4,11,384]{2,1,0:T(8,128)(2,1)S(1)} %get-tuple-element.225), channel_id=1, source_target_pairs={{4,0},{8,4},{12,8},{16,12},{20,16},{24,20},{28,24},{5,1},{9,5},{13... | collective-permute-start | bytes 101384 | tf_op jit(solution)/shard_map/ppermute | solution.py:249
  184.3 10.9 %collective-permute-start.2 = (bf16[4,11,384]{2,1,0:T(8,128)(2,1)S(1)}, bf16[4,11,384]{2,1,0:T(8,128)(2,1)S(1)}, u32[]{:S(2)}, u32[]{:S(2)}) collective-permute-start(bf16[4,11,384]{2,1,0:T(8,128)(2,1)S(1)} %get-tuple-element.226), channel_id=1, source_target_pairs={{0,4},{4,8},{8,12},{12,16},{16,20},{20,24},{24,28},{1,5},{5,9},{9,... | collective-permute-start | bytes 101384 | tf_op jit(solution)/shard_map/ppermute | solution.py:248
  193.6 39.1 %collective-permute-start.5 = (f32[512,384]{1,0:T(8,128)}, f32[512,384]{1,0:T(8,128)}, u32[]{:S(2)}, u32[]{:S(2)}) collective-permute-start(f32[512,384]{1,0:T(8,128)} %get-tuple-element.128), channel_id=1, source_target_pairs={{0,8},{8,0},{1,9},{9,1},{2,10},{10,2},{3,11},{11,3},{4,12},{12,4},... | collective-permute-start | bytes 2359304 | tf_op jit(solution)/shard_map/ppermute | solution.py:51
  195.2 36.6 %collective-permute-start.6 = (f32[512,384]{1,0:T(8,128)}, f32[512,384]{1,0:T(8,128)S(1)}, u32[]{:S(2)}, u32[]{:S(2)}) collective-permute-start(f32[512,384]{1,0:T(8,128)} %get-tuple-element.132), channel_id=1, source_target_pairs={{0,16},{16,0},{1,17},{17,1},{2,18},{18,2},{3,19},{19,3},{4,20},{20... | collective-permute-start | bytes 2359304 | tf_op jit(solution)/shard_map/ppermute | solution.py:51
  205.5 25.6 %all-to-all-start.3 = ((f32[32,1,1536]{2,1,0:T(1,128)}), f32[32,1,1536]{2,1,0:T(1,128)S(1)}, u32[]{:S(2)}, u32[]{:S(2)}) async-start(f32[32,1,1536]{2,1,0:T(1,128)} %broadcast_in_dim.29), calls=%async_computation.3 | async-start | bytes 393216 | tf_op jit(solution)/shard_map/all_to_all | solution.py:45
  208.6 94.7 %reduce-scatter.8.cloned.1.call-start = ((), (), s32[]{:S(2)}) async-start(), calls=%async_computation.9 | async-start | bytes 1720320 | tf_op jit(solution)/shard_map/reduce_scatter | solution.py:657
  236.6 15.9 %collective-permute-start.8 = (f32[256,384]{1,0:T(8,128)}, f32[256,384]{1,0:T(8,128)S(1)}, u32[]{:S(2)}, u32[]{:S(2)}) collective-permute-start(f32[256,384]{1,0:T(8,128)} %get-tuple-element.143), channel_id=1, source_target_pairs={{0,8},{8,0},{1,9},{9,1},{2,10},{10,2},{3,11},{11,3},{4,12},{12,4},... | collective-permute-start | bytes 1179656 | tf_op jit(solution)/shard_map/ppermute | solution.py:51
  236.7 16.0 %collective-permute-start.7 = (f32[256,384]{1,0:T(8,128)}, f32[256,384]{1,0:T(8,128)}, u32[]{:S(2)}, u32[]{:S(2)}) collective-permute-start(f32[256,384]{1,0:T(8,128)} %get-tuple-element.139), channel_id=1, source_target_pairs={{0,16},{16,0},{1,17},{17,1},{2,18},{18,2},{3,19},{19,3},{4,20},{20... | collective-permute-start | bytes 1179656 | tf_op jit(solution)/shard_map/ppermute | solution.py:51
  258.6 80.0 %all-gather.3.cloned.1.call-start = ((), (), s32[]{:S(2)}) async-start(), calls=%async_computation.10 | async-start | bytes 1720320 | tf_op jit(solution)/shard_map/all_gather | solution.py:658
  260.3 14.9 %collective-permute-start.9 = (f32[128,384]{1,0:T(8,128)S(1)}, f32[128,384]{1,0:T(8,128)S(1)}, u32[]{:S(2)}, u32[]{:S(2)}) collective-permute-start(f32[128,384]{1,0:T(8,128)S(1)} %copy-done.43), channel_id=1, source_target_pairs={{0,1},{1,0},{2,3},{3,2},{4,5},{5,4},{6,7},{7,6},{8,9},{9,8},{10,11... | collective-permute-start | bytes 589832 | tf_op jit(solution)/shard_map/ppermute | solution.py:51
  278.6 17.3 %collective-permute-start.12 = (f32[64,384]{1,0:T(8,128)}, f32[64,384]{1,0:T(8,128)S(1)}, u32[]{:S(2)}, u32[]{:S(2)}) collective-permute-start(f32[64,384]{1,0:T(8,128)} %get-tuple-element.169), channel_id=1, source_target_pairs={{0,2},{1,3},{2,0},{3,1},{4,6},{5,7},{6,4},{7,5},{8,10},{9,11},{10,... | collective-permute-start | bytes 294920 | tf_op jit(solution)/shard_map/ppermute | solution.py:51
  282.7 17.2 %collective-permute-start.11 = (f32[64,384]{1,0:T(8,128)}, f32[64,384]{1,0:T(8,128)S(1)}, u32[]{:S(2)}, u32[]{:S(2)}) collective-permute-start(f32[64,384]{1,0:T(8,128)} %get-tuple-element.168), channel_id=1, source_target_pairs={{0,2},{1,3},{2,0},{3,1},{4,6},{5,7},{6,4},{7,5},{8,10},{9,11},{10,... | collective-permute-start | bytes 294920 | tf_op jit(solution)/shard_map/ppermute | solution.py:51
  303.3 110.9 %all-gather.5.cloned.1.call-start = ((), (), s32[]{:S(2)}) async-start(), calls=%async_computation.11 | async-start | bytes 12386304 | tf_op jit(solution)/shard_map/all_gather | solution.py:658
  312.8 10.9 %collective-permute-start.16 = (bf16[128,384]{1,0:T(8,128)(2,1)}, bf16[128,384]{1,0:T(8,128)(2,1)S(1)}, u32[]{:S(2)}, u32[]{:S(2)}) collective-permute-start(bf16[128,384]{1,0:T(8,128)(2,1)} %get-tuple-element.188.refs_2_), channel_id=1, source_target_pairs={{0,1},{1,0},{2,3},{3,2},{4,5},{5,4},{6,7},{7,6},{8,9},{9,8},{10,11... | collective-permute-start | bytes 294920 | tf_op jit(solution)/shard_map/ppermute | solution.py:51
  314.1 15.3 %collective-permute-start.15 = (bf16[128,384]{1,0:T(8,128)(2,1)}, bf16[128,384]{1,0:T(8,128)(2,1)S(1)}, u32[]{:S(2)}, u32[]{:S(2)}) collective-permute-start(bf16[128,384]{1,0:T(8,128)(2,1)} %get-tuple-element.187.refs_0_), channel_id=1, source_target_pairs={{0,1},{1,0},{2,3},{3,2},{4,5},{5,4},{6,7},{7,6},{8,9},{9,8},{10,11... | collective-permute-start | bytes 294920 | tf_op jit(solution)/shard_map/ppermute | solution.py:51
  350.7 19.8 %collective-permute-start.20 = (bf16[512,384]{1,0:T(8,128)(2,1)}, bf16[512,384]{1,0:T(8,128)(2,1)S(1)}, u32[]{:S(2)}, u32[]{:S(2)}) collective-permute-start(bf16[512,384]{1,0:T(8,128)(2,1)} %get-tuple-element.197.refs_2_), channel_id=1, source_target_pairs={{0,16},{16,0},{1,17},{17,1},{2,18},{18,2},{3,19},{19,3},{4,20},{20... | collective-permute-start | bytes 1179656 | tf_op jit(solution)/shard_map/ppermute | solution.py:51
  352.1 19.7 %collective-permute-start.19 = (bf16[512,384]{1,0:T(8,128)(2,1)}, bf16[512,384]{1,0:T(8,128)(2,1)S(1)}, u32[]{:S(2)}, u32[]{:S(2)}) collective-permute-start(bf16[512,384]{1,0:T(8,128)(2,1)} %get-tuple-element.196.refs_0_), channel_id=1, source_target_pairs={{0,8},{8,0},{1,9},{9,1},{2,10},{10,2},{3,11},{11,3},{4,12},{12,4},... | collective-permute-start | bytes 1179656 | tf_op jit(solution)/shard_map/ppermute | solution.py:51
  (55 other events, 284.1 us)
Sparse Core Ops, SparseCore 0:
  90.7 54.3 reduce-scatter.5
  165.9 84.3 reduce-scatter.3
  258.7 39.2 reduce-scatter.7
  303.4 35.2 all-gather.2
  340.6 73.5 all-gather.4

commit v2 on v1

--- a/solution.py
+++ b/solution.py
@@ -135,10 +135,9 @@
 
 
 class Group:
-    def __init__(self, order, pieces, rows, base, routes):
-        self.order = order
+    def __init__(self, pieces, rows, routes):
         self.parts = [
-            {"pieces": [(piece, at + base) for piece in pieces], "rows": count, "route": route}
+            {"pieces": [(piece, at) for piece in pieces], "rows": count, "route": route}
             for at, count, route in zip(
                 [sum(rows[:i]) for i in range(len(rows))], rows, routes
             )
@@ -148,64 +147,52 @@
         self.flying = None
         self.shares = None
 
-    def moved(self, values, level):
-        self.flying = [
-            swap(value, part["route"][level]) for value, part in zip(values, self.parts)
-        ]
-
     def work(self, arrays, flying):
         level = self.level
-        parts = self.parts
-        if level <= self.levels:
-            wanted = []
-            for i, part in enumerate(parts):
-                pieces = list(zip(arrays[i], [at for _, at in part["pieces"]]))
-                if level:
-                    mine = upper(part["route"][level - 1])
-                    pieces = [(a, at + mine * part["rows"]) for a, at in pieces]
-                    pieces.append((flying[i], 0))
-                part["pieces"] = pieces
-                if level < self.levels:
-                    part["rows"] //= 2
-                    away = 1 - upper(part["route"][level])
-                    pieces = [(a, at + away * part["rows"]) for a, at in pieces]
-                wanted.append((part["rows"], pieces))
-            return sum_parts(wanted, F32 if level < self.levels else BF16)
-        back = 2 * self.levels - level
-        return join_parts(
-            [
-                (share, arrived, upper(part["route"][back]))
-                for share, arrived, part in zip(self.shares, flying, parts)
-            ],
-            stacked=level == 2 * self.levels,
-        )
-
-    def step(self):
-        if self.done():
-            return
+        if level > self.levels:
+            back = 2 * self.levels - level
+            return join_parts(
+                [
+                    (share, arrived, upper(part["route"][back]))
+                    for share, arrived, part in zip(self.shares, flying, self.parts)
+                ],
+                stacked=level == 2 * self.levels,
+            )
+        wanted = []
+        for i, part in enumerate(self.parts):
+            pieces = list(zip(arrays[i], [at for _, at in part["pieces"]]))
+            if level:
+                mine = upper(part["route"][level - 1])
+                pieces = [(a, at + mine * part["rows"]) for a, at in pieces]
+                pieces.append((flying[i], 0))
+            part["pieces"] = pieces
+            if level < self.levels:
+                part["rows"] //= 2
+                away = 1 - upper(part["route"][level])
+                pieces = [(a, at + away * part["rows"]) for a, at in pieces]
+            wanted.append((part["rows"], pieces))
+        return sum_parts(wanted, F32 if level < self.levels else BF16)
+
+    def step(self, held=()):
         arrays = [[a for a, _ in part["pieces"]] for part in self.parts]
-        values = self.order.run(self.work, arrays, self.flying)
+        values = self.work(arrays, self.flying)
+        values, held = tie(values, held)
         if self.level >= self.levels:
             self.shares = values
-        if self.level < self.levels:
-            self.moved(values, self.level)
-        elif self.level < 2 * self.levels:
-            self.moved(values, 2 * self.levels - 1 - self.level)
+        if self.level < 2 * self.levels:
+            next_level = min(self.level, 2 * self.levels - 1 - self.level)
+            self.flying = [
+                swap(value, part["route"][next_level]) for value, part in zip(values, self.parts)
+            ]
         self.level += 1
+        return held
 
     def done(self):
         return self.level > 2 * self.levels
 
 
-class Order:
-    def __init__(self):
-        self.token = ()
-
-    def run(self, work, *given):
-        given, _ = lax.optimization_barrier((given, self.token))
-        result = work(*given)
-        self.token = jax.tree.leaves(result)[:1]
-        return result
+def tie(*values):
+    return lax.optimization_barrier(values)
 
 
 def gelu_pair(values):
@@ -264,7 +251,6 @@
     species_ref,
     windows_ref,
     humans_ref,
-    core_ref,
     mouse_ref,
     human_ref,
     bias_mouse_ref,
@@ -272,25 +258,28 @@
     counts_ref,
     rows_ref,
     columns_ref,
-    *refs,
+    out_ref,
+    grads_ref,
+    bias_grad_ref,
+    weight_ref,
+    bias_ref,
+    sums_ref,
+    *,
     mouse_tiles,
-    first_human,
     tracks,
     scales,
 ):
-    *out_refs, grads_ref, bias_grad_ref, weight_ref, bias_ref, sums_ref, total_ref = refs
     step = pl.program_id(0)
     tile, width = weight_ref.shape
     windows = windows_ref.shape[0]
     span = rows_ref.shape[0] // windows
     lane = counts_ref.shape[1]
     groups = span // lane
-    half = width // 2
     is_mouse = step < mouse_tiles
     humans = humans_ref[0]
     active = jnp.where(is_mouse, windows - humans, humans)
     skipped = jnp.where(is_mouse, humans, 0)
-    first = jnp.where(is_mouse, step, first_human + step - mouse_tiles) * tile
+    first = jnp.where(is_mouse, step, step - mouse_tiles) * tile
     end = jnp.where(is_mouse, tracks[1], tracks[0])
     scale = jnp.where(is_mouse, scales[1], scales[0]).astype(F32)
 
@@ -307,7 +296,7 @@
             weight_ref[...] = jnp.where(inside, human_ref[...], BF16(0))
             bias_ref[...] = jnp.broadcast_to(bias_human_ref[...], (LANES, tile)).T
 
-    def slopes(logits, window):
+    def slopes(logits, window, scale):
         inside = first + lax.broadcasted_iota(jnp.int32, (tile, 1), 0) < end
         total = jnp.zeros((tile, lane), F32)
         low = []
@@ -321,50 +310,41 @@
             low.append(slope.astype(BF16))
         return total, jnp.concatenate(low, axis=1)
 
-    def store(product):
-        if len(out_refs) == 1:
-            out_refs[0][...] = product
-            return
-        mine = core_ref[0] == 0
-        out_refs[0][...] = jnp.where(mine, product[:, :half], product[:, half:])
-        out_refs[1][...] = jnp.where(mine, product[:, half:], product[:, :half])
-
     @pl.when(active == 0)
     def _():
-        for out_ref in out_refs:
-            out_ref[...] = jnp.zeros_like(out_ref)
+        out_ref[...] = jnp.zeros_like(out_ref)
         grads_ref[...] = jnp.zeros_like(grads_ref)
         bias_grad_ref[...] = jnp.zeros_like(bias_grad_ref)
 
-    @pl.when(active == windows)
+    @pl.when(active * 4 >= windows * 3)
     def _():
         prepare()
         total = None
         for i in range(windows):
             lanes = slice(i * span, (i + 1) * span)
             logits = jnp.dot(weight_ref[...], columns_ref[:, lanes], preferred_element_type=F32)
-            part, low = slopes(logits, i)
+            part, low = slopes(
+                logits, i, jnp.where((species_ref[i] == 1) == is_mouse, scale, 0.0)
+            )
             total = part if total is None else total + part
             grads_ref[:, lanes] = low
         bias_grad_ref[...] = jnp.sum(total.T, axis=0, keepdims=True)
         product = jnp.dot(grads_ref[...], rows_ref[...], preferred_element_type=F32)
-        store(product.astype(BF16))
-
-    @pl.when((active > 0) & (active < windows))
+        out_ref[...] = product.astype(BF16)
+
+    @pl.when((active > 0) & (active * 4 < windows * 3))
     def _():
         prepare()
         grads_ref[...] = jnp.zeros_like(grads_ref)
         sums_ref[...] = jnp.zeros_like(sums_ref)
-        total_ref[...] = jnp.zeros_like(total_ref)
 
         def one(window):
             at = window * span
             lanes = pl.ds(at if isinstance(window, int) else pl.multiple_of(at, span), span)
             logits = jnp.dot(weight_ref[...], columns_ref[:, lanes], preferred_element_type=F32)
-            part, low = slopes(logits, window)
+            part, low = slopes(logits, window, scale)
             sums_ref[...] += part
             grads_ref[:, lanes] = low
-            total_ref[...] += jnp.dot(low, rows_ref[lanes, :], preferred_element_type=F32)
             return 0
 
         if span % LANES == 0:
@@ -376,30 +356,27 @@
                 def _():
                     one(i)
         bias_grad_ref[...] = jnp.sum(sums_ref[...].T, axis=0, keepdims=True)
-        store(total_ref[...].astype(BF16))
+        product = jnp.dot(grads_ref[...], rows_ref[...], preferred_element_type=F32)
+        out_ref[...] = product.astype(BF16)
 
 
 def head(
-    species, order, humans, core, mouse, human, bias_mouse, bias_human, counts, rows, columns, scales,
-    mouse_tiles, first_human, human_tiles, split,
+    species, order, humans, mouse, human, bias_mouse, bias_human, counts, rows, columns, scales
 ):
     tokens, width = rows.shape
     lane = counts.shape[1]
     tracks = (human.shape[0], mouse.shape[0])
-    tiles = mouse_tiles + human_tiles
-    at_mouse = lambda j: jnp.minimum(j, max(mouse_tiles - 1, 0))
-    at_human = lambda j: first_human + jnp.maximum(j - mouse_tiles, 0)
-    at_both = lambda j: jnp.where(j < mouse_tiles, j, first_human + j - mouse_tiles)
+    mouse_tiles = pl.cdiv(tracks[1], TILE)
+    tiles = mouse_tiles + pl.cdiv(tracks[0], TILE)
+    at_mouse = lambda j: jnp.minimum(j, mouse_tiles - 1)
+    at_human = lambda j: jnp.maximum(j - mouse_tiles, 0)
+    at_both = lambda j: jnp.where(j < mouse_tiles, j, j - mouse_tiles)
     fixed = lambda j, *_: (0, 0)
     out = lambda j, *_: (j, 0)
-    strip = width // 2 if split else width
-    copies = 2 if split else 1
     return pl.pallas_call(
-        functools.partial(
-            head_body, mouse_tiles=mouse_tiles, first_human=first_human, tracks=tracks, scales=scales
-        ),
+        functools.partial(head_body, mouse_tiles=mouse_tiles, tracks=tracks, scales=scales),
         grid_spec=pltpu.PrefetchScalarGridSpec(
-            num_scalar_prefetch=4,
+            num_scalar_prefetch=3,
             grid=(tiles,),
             in_specs=[
                 pl.BlockSpec((TILE, width), lambda j, *_: (at_mouse(j), 0)),
@@ -410,17 +387,19 @@
                 pl.BlockSpec((tokens, width), fixed),
                 pl.BlockSpec((width, tokens), fixed),
             ],
-            out_specs=[pl.BlockSpec((TILE, strip), out)] * copies
-            + [pl.BlockSpec((TILE, tokens), out), pl.BlockSpec((1, TILE), lambda j, *_: (0, j))],
+            out_specs=[
+                pl.BlockSpec((TILE, width), out),
+                pl.BlockSpec((TILE, tokens), out),
+                pl.BlockSpec((1, TILE), lambda j, *_: (0, j)),
+            ],
             scratch_shapes=[
                 pltpu.VMEM((TILE, width), BF16),
                 pltpu.VMEM((TILE, LANES), F32),
                 pltpu.VMEM((TILE, lane), F32),
-                pltpu.VMEM((TILE, width), F32),
             ],
         ),
-        out_shape=[jax.ShapeDtypeStruct((tiles * TILE, strip), BF16)] * copies
-        + [
+        out_shape=[
+            jax.ShapeDtypeStruct((tiles * TILE, width), BF16),
             jax.ShapeDtypeStruct((tiles * TILE, tokens), BF16),
             jax.ShapeDtypeStruct((1, tiles * TILE), F32),
         ],
@@ -430,12 +409,11 @@
             bytes_accessed=tiles * TILE * (tokens * 6 + width * 4),
             transcendentals=3 * tiles * TILE * tokens,
         ),
-    )(species, order, humans, core, mouse, human, bias_mouse, bias_human, counts, rows, columns)
+    )(species, order, humans, mouse, human, bias_mouse, bias_human, counts, rows, columns)
 
 
 def back_body(
-    humans_ref, mouse_ref, human_ref, early_ref, late_ref, out_ref, total_ref,
-    *, mouse_tiles, early_tiles, tracks, windows,
+    humans_ref, mouse_ref, human_ref, grads_ref, out_ref, total_ref, *, mouse_tiles, tracks, windows
 ):
     step = pl.program_id(0)
     tile = mouse_ref.shape[0]
@@ -450,39 +428,28 @@
     def _():
         inside = step * tile + row < tracks[1]
         weight = jnp.where(inside, mouse_ref[...], BF16(0)).T
-        total_ref[...] += jnp.dot(weight, early_ref[...], preferred_element_type=F32)
-
-    def human(grads_ref):
+        total_ref[...] += jnp.dot(weight, grads_ref[...], preferred_element_type=F32)
+
+    @pl.when((step >= mouse_tiles) & (humans_ref[0] > 0))
+    def _():
         inside = (step - mouse_tiles) * tile + row < tracks[0]
         weight = jnp.where(inside, human_ref[...], BF16(0)).T
         total_ref[...] += jnp.dot(weight, grads_ref[...], preferred_element_type=F32)
 
-    some = humans_ref[0] > 0
-
-    @pl.when((step >= mouse_tiles) & (step < early_tiles) & some)
-    def _():
-        human(early_ref)
-
-    @pl.when((step >= early_tiles) & some)
-    def _():
-        human(late_ref)
-
     @pl.when(step == pl.num_programs(0) - 1)
     def _():
         out_ref[...] = total_ref[...].T
 
 
-def head_back(humans, windows, mouse, human, early, late):
-    tokens = early.shape[1]
+def head_back(humans, windows, mouse, human, grads):
+    tokens = grads.shape[1]
     width = human.shape[1]
     mouse_tiles = pl.cdiv(mouse.shape[0], TILE)
-    early_tiles = early.shape[0] // TILE
-    tiles = early_tiles + late.shape[0] // TILE
+    tiles = grads.shape[0] // TILE
     return pl.pallas_call(
         functools.partial(
             back_body,
             mouse_tiles=mouse_tiles,
-            early_tiles=early_tiles,
             tracks=(human.shape[0], mouse.shape[0]),
             windows=windows,
         ),
@@ -492,8 +459,7 @@
             in_specs=[
                 pl.BlockSpec((TILE, width), lambda j, *_: (jnp.minimum(j, mouse_tiles - 1), 0)),
                 pl.BlockSpec((TILE, width), lambda j, *_: (jnp.maximum(j - mouse_tiles, 0), 0)),
-                pl.BlockSpec((TILE, tokens), lambda j, *_: (jnp.minimum(j, early_tiles - 1), 0)),
-                pl.BlockSpec((TILE, tokens), lambda j, *_: (jnp.maximum(j - early_tiles, 0), 0)),
+                pl.BlockSpec((TILE, tokens), lambda j, *_: (j, 0)),
             ],
             out_specs=pl.BlockSpec((tokens, width), lambda j, *_: (0, 0)),
             scratch_shapes=[pltpu.VMEM((width, tokens), F32)],
@@ -505,21 +471,19 @@
             bytes_accessed=tiles * TILE * (tokens + width) * 2,
             transcendentals=0,
         ),
-    )(humans, mouse, human, early, late)
+    )(humans, mouse, human, grads)
 
 
 def widen_body(in_ref, out_ref):
     out_ref[...] = in_ref[0].astype(F32)
 
 
-def widen_head(tracks, summed, before, early):
-    devices, rows, width = summed.shape
-    block = rows // 2
-    place = lambda j: (jnp.where(j < early, before + j, j - early), jnp.where(j < early, 0, 1), 0)
+def widen_head(tracks, summed, first):
+    _, block, width = summed.shape
     return pl.pallas_call(
         widen_body,
         grid=(pl.cdiv(tracks, block),),
-        in_specs=[pl.BlockSpec((1, block, width), place)],
+        in_specs=[pl.BlockSpec((1, block, width), lambda j: (first // block + j, 0, 0))],
         out_specs=pl.BlockSpec((block, width), lambda j: (j, 0)),
         out_shape=jax.ShapeDtypeStruct((tracks, width), F32),
         compiler_params=pltpu.CompilerParams(vmem_limit_bytes=60 * 2**20),
@@ -644,41 +608,20 @@
     by_species = jnp.argsort(species).astype(jnp.int32)
     humans = jnp.sum(species == 0).astype(jnp.int32)[None]
     mouse_tiles, human_tiles = pl.cdiv(tracks_mouse, TILE), pl.cdiv(tracks_human, TILE)
-    early_tiles = (mouse_tiles + human_tiles) // 2 - mouse_tiles
-    late_tiles = human_tiles - early_tiles
     mouse, human = head_mouse.T, head_human.T
 
-    def some_tiles(*which):
-        return head(
-            species, by_species, humans, core, mouse, human, bias_mouse[None], bias_human[None],
-            counts_rows, block_out, columns, scales, *which,
-        )
-
     scatter = lambda value, axes: lax.psum_scatter(value, axes, scatter_dimension=0, tiled=True)
-    gather = lambda value, axes: lax.all_gather(value, axes, axis=0, tiled=True)
+    gather = lambda value, axes: lax.all_gather(value, axes)
     across, along, deep = bits_of("x"), bits_of("y"), bits_of("batch")
-    order = Order()
-    early, slopes_early, bias_early = some_tiles(mouse_tiles, 0, early_tiles, False)
-    order.token = [bias_early]
-    early = scatter(early, BINS)
-    late, slopes_late, bias_late = order.run(
-        lambda *_: some_tiles(0, early_tiles, late_tiles, False), bias_early
-    )
-    order.token = [bias_late]
-    late = scatter(late, BINS)
-    output_grad = order.run(
-        lambda early, late: head_back(humans, windows, mouse, human, early, late),
-        slopes_early,
-        slopes_late,
-    )
+    grads, slopes, bias_grads = head(
+        species, by_species, humans, mouse, human, bias_mouse[None], bias_human[None],
+        counts_rows, block_out, columns, scales,
+    )
+    summed = scatter(grads, BINS)
+    output_grad = head_back(humans, windows, mouse, human, slopes)
     to_core = lambda value: swap(value, CORE)
     chips = lax.axis_size(CHIPS)
     unit = 16 * chips
-
-    def cut(rows, count):
-        count = min(count, rows // unit)
-        ends = [rows // unit * (i + 1) // count * unit for i in range(count)]
-        return [end - start for end, start in zip(ends, [0] + ends[:-1])]
 
     def after_head(output_grad):
         branch_grad = output_grad.astype(BF16)
@@ -686,14 +629,14 @@
         sent, _ = small_sum([jnp.sum(mid_grad, axis=0), jnp.sum(mid_grad * normed_mid, axis=0)])
         return sent, branch_grad, mid_grad
 
-    sent, branch_grad, mid_grad = order.run(after_head, output_grad)
+    sent, branch_grad, mid_grad = after_head(output_grad)
     everyone = to_all(sent)
 
     def weight_work(branch_grad, output_grad):
         product = rows_product(hidden_mid, branch_grad).reshape(middle, width // middle, middle)
         return product.swapaxes(0, 1).reshape(-1, middle), jnp.sum(output_grad, axis=0)
 
-    proj_grad, proj_bias_grad = order.run(weight_work, branch_grad, output_grad)
+    proj_grad, proj_bias_grad = weight_work(branch_grad, output_grad)
 
     def middle_work(everyone, mid_grad):
         _, finish = small_sum([shift_mid, gain_mid])
@@ -703,15 +646,14 @@
         )
         return dilated_grad.astype(BF16), shift_mid_grad, gain_mid_grad
 
-    dilated_grad, shift_mid_grad, gain_mid_grad = order.run(middle_work, everyone, mid_grad)
+    dilated_grad, shift_mid_grad, gain_mid_grad = middle_work(everyone, mid_grad)
     dilated_windows = dilated_grad.reshape(windows, span, middle)
     grad_before, grad_after = [move(value) for value, move in edges(dilated_windows, DILATION_STEP)]
     sums = jnp.concatenate(
         [
             proj_bias_grad,
-            bias_early[0, mouse_tiles * TILE :],
-            bias_late[0, : tracks_human - early_tiles * TILE],
-            bias_early[0, :tracks_mouse],
+            bias_grads[0, mouse_tiles * TILE : mouse_tiles * TILE + tracks_human],
+            bias_grads[0, :tracks_mouse],
         ]
     )
     weight_rows = pl.cdiv(4 * width * middle + sums.size, middle)
@@ -725,17 +667,15 @@
         grads = jnp.concatenate(parts, axis=0)
         return lax.dynamic_slice_in_dim(grads, (1 - core[0]) * half, half, 0), grads
 
-    weights_send, weights_grad = order.run(conv_work, dilated_grad, proj_grad, sums)
+    weights_send, weights_grad = conv_work(dilated_grad, proj_grad, sums)
     weights_arrived = to_core(weights_send)
     weights_keep = lax.dynamic_slice_in_dim(weights_grad, core[0] * half, half, 0)
     weights = Group(
-        order,
         [weights_keep, weights_arrived],
-        cut(half, 2),
-        0,
+        [half // 2] * 2,
         (across + along + deep, along + across + deep),
     )
-    weights.step()
+    grad_before = weights.step(grad_before)
 
     def hidden_work(grad_before, dilated_windows, grad_after):
         grad_shifted = taps(
@@ -748,9 +688,16 @@
         sent, _ = small_sum([jnp.sum(in_grad, axis=0), jnp.sum(in_grad * normed_in, axis=0)])
         return sent, in_grad
 
-    sent, in_grad = order.run(hidden_work, grad_before, dilated_windows, grad_after)
+    sent, in_grad = hidden_work(grad_before, dilated_windows, grad_after)
     everyone = to_all(sent)
+    summed, in_grad = tie(summed, in_grad)
+    summed = scatter(summed, "batch")
     weights.step()
+    everyone = weights.step(everyone)
+    summed = weights.step(summed)
+    summed = gather(summed, "batch").reshape(-1, width)
+    summed = weights.step(summed)
+    summed = gather(summed, BINS)
 
     def last_work(everyone, output_grad, in_grad):
         _, finish = small_sum([shift_in, gain_in])
@@ -760,37 +707,21 @@
         )
         return input_grad.astype(BF16), shift_in_grad, gain_in_grad
 
-    input_grad, shift_in_grad, gain_in_grad = order.run(last_work, everyone, output_grad, in_grad)
-    weights.step()
-    summed = order.run(lambda *both: jnp.concatenate(both, axis=0), early, late)
-    summed = scatter(summed, "batch")
-    weights.step()
-    weights.step()
-    summed = gather(order.run(lambda value: value, summed), "batch")
-    weights.step()
-    weights.step()
-    summed = gather(order.run(lambda value: value, summed), BINS)
+    input_grad, shift_in_grad, gain_in_grad = last_work(everyone, output_grad, in_grad)
     while not weights.done():
         weights.step()
-    summed = summed.reshape(lax.axis_size(BINS), -1, width)
     weights_mine = weights.shares[0]
-    weights_other = to_core(weights_mine)
-    conv_total, proj_total, sums_total = order.run(
-        lambda mine, other: finish_weights(core, mine, other, 3 * width, (middle, width)),
-        weights_mine,
-        weights_other,
-    )
-    conv_total = conv_total.reshape(3, width, middle)
+    conv_total, proj_total, sums_total = finish_weights(
+        core, weights_mine, to_core(weights_mine), 3 * width, (middle, width)
+    )
     conv_total = conv_total.reshape(3, width, middle)
     sums_total = sums_total.reshape(-1)
     ends = [0, width, width + tracks_human, width + tracks_human + tracks_mouse]
     proj_bias_total, bias_human_grad, bias_mouse_grad = [
         sums_total[low:high] for low, high in zip(ends[:-1], ends[1:])
     ]
-    per_tile = TILE // (summed.shape[1] // 2)
-    mouse_blocks, early_blocks = mouse_tiles * per_tile, early_tiles * per_tile
-    head_mouse_grad = widen_head(tracks_mouse, summed, 0, mouse_blocks)
-    head_human_grad = widen_head(tracks_human, summed, mouse_blocks, early_blocks)
+    head_mouse_grad = widen_head(tracks_mouse, summed, 0)
+    head_human_grad = widen_head(tracks_human, summed, mouse_tiles * TILE)
     return (
         block_out.reshape(windows, span, width),
         input_grad.reshape(windows, span, width),

time: 445 us -> 385 us (0.87)
  waiting for transfers between devices: 152 us -> 114 us
  Pallas kernels: 140 us -> 115 us
    pallas_call x3 -> x2, Pallas kernels: 90.2 us -> 70.5 us  [the longest x1 49 us: head(): pl.pallas_call(functools.partial(head_body, mouse_tiles=mouse_tiles, trac...]
    all_to_all x4, waiting for transfers between devices: 38.4 us -> 22.5 us  [to_all(): return lax.all_to_all(sent, axes, 0, 0, tiled=True)]
    all_gather x2, waiting for transfers between devices: 29.6 us -> 14.1 us  [on_device(): gather = lambda value, axes: lax.all_gather(value, axes)]
    ppermute x18, waiting for transfers between devices: 83.6 us -> 73.5 us  [swap(): return lax.ppermute(value, axis, [(i, i ^ mask) for i in range(size)])]
    all_to_all x4, starting transfers between devices: 15.5 us -> 20.6 us  [to_all(): return lax.all_to_all(sent, axes, 0, 0, tiled=True)]
    unnamed x100 -> x92, local copies, waits for them, and re-layouts: 15.5 us -> 14.5 us
  transfers between devices with their start and end apart: 31 -> 30, of which waited for: 20 -> 20; matrix products, arithmetic and copies ran while one was open for 13% -> 15% of each run, Pallas kernels for 20% -> 14%
where the time goes in v2:
time: 385 us; the launch traced here: 378 us
  Pallas kernels  115 us (30%)
  waiting for transfers between devices  114 us (30%)
  starting transfers between devices  48.3 us (13%)
  local copies, waits for them, and re-layouts  36.4 us (9%)
  matrix products  25.9 us (7%)
  other arithmetic  23.4 us (6%)
  between operations  14.8 us (4%)
    ppermute x18, waiting for transfers between devices, swap(): return lax.ppermute(value, axis, [(i, i ^ mask) for i in range(size)])  73.5 us
    pallas_call x1, Pallas kernels, head(): pl.pallas_call(functools.partial(head_body, mouse_tiles=mouse_tiles, trac...  49 us
    all_to_all x4, waiting for transfers between devices, to_all(): return lax.all_to_all(sent, axes, 0, 0, tiled=True)  22.5 us
    pallas_call x1, Pallas kernels, head_back(): pl.pallas_call(functools.partial(back_body, mouse_tiles=mouse_tiles, trac...  21.4 us
    all_to_all x4, starting transfers between devices, to_all(): return lax.all_to_all(sent, axes, 0, 0, tiled=True)  20.6 us
    ppermute x18, starting transfers between devices, swap(): return lax.ppermute(value, axis, [(i, i ^ mask) for i in range(size)])  18.7 us
    pallas_call x5, Pallas kernels, sum_parts(): pl.pallas_call(functools.partial(sum_body, counts=counts), grid_spec=pltp...  15.2 us
    unnamed x92, local copies, waits for them, and re-layouts  14.5 us
  transfers between devices with their start and end apart: 30, of which 20 were waited for; matrix products, arithmetic and copies ran while one was open for 15% of the time, Pallas kernels for 14%

profile of v2, /device:TPU:0, one launch (start us, length us, event | category | flops | bytes accessed | tf_op | source)
XLA Modules:
  0.0 378.0 jit_solution(2424892287946478494)
XLA Ops:
  10.0 7.3 %all-to-all-start = ((f32[32,1,1536]{2,1,0:T(1,128)}), f32[32,1,1536]{2,1,0:T(1,128)S(1)}, u32[]{:S(2)}, u32[]{:S(2)}) async-start(f32[32,1,1536]{2,1,0:T(1,128)} %broadcast_in_dim.21), calls=%async_computation | async-start | bytes 393216 | tf_op jit(solution)/shard_map/all_to_all | solution.py:45
  21.7 4.9 %all-to-all-done = f32[32,1,1536]{2,1,0:T(1,128)S(1)} async-done(((f32[32,1,1536]{2,1,0:T(1,128)}), f32[32,1,1536]{2,1,0:T(1,128)S(1)}, u32[]{:S(2)}, u32[]{:S(2)}) %all-to-all-start) | async-done | bytes 196640 | tf_op jit(solution)/shard_map/all_to_all | solution.py:45
  40.4 5.3 %all-to-all-done.1 = f32[32,1,768]{2,1,0:T(1,128)S(1)} async-done(((f32[32,1,768]{2,1,0:T(1,128)}), f32[32,1,768]{2,1,0:T(1,128)S(1)}, u32[]{:S(2)}, u32[]{:S(2)}) %all-to-all-start.1) | async-done | bytes 98336 | tf_op jit(solution)/shard_map/all_to_all | solution.py:45
  45.9 3.9 %fusion.12.rows_ref = bf16[1024,768]{1,0:T(8,128)(2,1)} fusion(bf16[4,256,768]{2,1,0:T(8,128)(2,1)S(1)} %copy-done.3, bf16[384,768]{1,0:T(8,128)(2,1)S(1)} %copy-done, f32[768]{0:T(1024)S(1)} %copy-done.42, f32[1024,384]{1,0:T(8,128)} %get-tuple-element.119, f32[384]{0:T(512)S(1)} %copy-done.43, f32[384]{0:T(512)S(1)} %copy-done.41, ...), kind=kOutput, calls=%fused_computation.17 | convolution fusion | flops 611057664 | bytes 5317632 | tf_op jit(solution)/shard_map/dot_general | solution.py:596
  52.5 49.0 %shard_map.237 = (bf16[7168,768]{1,0:T(8,128)(2,1)}, bf16[7168,1024]{1,0:T(8,128)(2,1)}, f32[1,7168]{1,0:T(1,128)}) custom-call(s32[4]{0:T(128)} %species_ref.1, s32[4]{0:T(128)} %get-tuple-element.50.windows_ref, s32[1]{0:T(128)} %bitcast.8.humans_ref, bf16[1643,768]{1,0:T(8,128)(2,1)} %bitcast.160, bf16[5313,768]{1,0:T(8,128)(2,1)} %bitcast.157, ...), custom_call_target="tpu_custom_call" | custom-call | flops 22548578304 | bytes 66060288 | tf_op jit(solution)/shard_map/pallas_call | solution.py:376
  103.9 21.4 %shard_map.238 = f32[1024,768]{1,0:T(8,128)} custom-call(s32[1]{0:T(128)} %bitcast.8.humans_ref, bf16[1643,768]{1,0:T(8,128)(2,1)} %bitcast.161, bf16[5313,768]{1,0:T(8,128)(2,1)} %bitcast.158, bf16[7168,1024]{1,0:T(8,128)(2,1)} %get-tuple-element.51.grads_ref), custom_call_target="tpu_custom_call" | custom-call | flops 11274289152 | bytes 25690112 | tf_op jit(solution)/shard_map/pallas_call | solution.py:449
  134.4 5.8 %all-to-all-start.2 = ((f32[32,1,768]{2,1,0:T(1,128)}), f32[32,1,768]{2,1,0:T(1,128)S(1)}, u32[]{:S(2)}, u32[]{:S(2)}) async-start(f32[32,1,768]{2,1,0:T(1,128)} %broadcast_in_dim.27), calls=%async_computation.3 | async-start | bytes 196608 | tf_op jit(solution)/shard_map/all_to_all | solution.py:45
  144.6 3.7 all-to-all-done.2
  165.7 4.0 %fusion.33 = f32[1024,768]{1,0:T(8,128)} fusion(bf16[1024,384]{1,0:T(8,128)(2,1)} %copy-done.8, bf16[3,768,384]{2,1,0:T(8,128)(2,1)} %param.17), kind=kOutput, calls=%fused_computation.57 | convolution fusion | flops 603979776 | bytes 4521984 | tf_op jit(solution)/shard_map/dot_general | solution.py:210
  171.3 3.8 shard_map.239
  178.6 4.1 %fusion.52 = (f32[768]{0:T(1024)S(1)}, f32[768]{0:T(1024)S(1)}, f32[1024,768]{1,0:T(8,128)}) fusion(f32[768]{0:T(1024)S(1)} %get-tuple-element.113, f32[768]{0:T(1024)S(1)} %get-tuple-element.112, bf16[4,256,768]{2,1,0:T(8,128)(2,1)S(1)} %copy-done.4, f32[768]{0:T(1024)S(1)} %copy-done.35, f32[768]{0:T(1024)S(1)} %copy-done.32, ...), kind=kOutput, calls=%fused_computation.102 | convolution fusion | flops 618920448 | bytes 12408832 | tf_op jit(solution)/shard_map/dot_general | solution.py:210
  188.5 17.2 %collective-permute-done.5.refs_2_ = f32[512,384]{1,0:T(8,128)S(1)} collective-permute-done((f32[512,384]{1,0:T(8,128)}, f32[512,384]{1,0:T(8,128)S(1)}, u32[]{:S(2)}, u32[]{:S(2)}) %collective-permute-start.5) | collective-permute-done | bytes 786464 | tf_op jit(solution)/shard_map/ppermute | solution.py:51
  213.3 4.6 %all-to-all-start.3 = ((f32[32,1,1536]{2,1,0:T(1,128)}), f32[32,1,1536]{2,1,0:T(1,128)S(1)}, u32[]{:S(2)}, u32[]{:S(2)}) async-start(f32[32,1,1536]{2,1,0:T(1,128)} %broadcast_in_dim.28), calls=%async_computation.4 | async-start | bytes 393216 | tf_op jit(solution)/shard_map/all_to_all | solution.py:45
  218.6 8.6 %all-to-all-done.3 = f32[32,1,1536]{2,1,0:T(1,128)S(1)} async-done(((f32[32,1,1536]{2,1,0:T(1,128)}), f32[32,1,1536]{2,1,0:T(1,128)S(1)}, u32[]{:S(2)}, u32[]{:S(2)}) %all-to-all-start.3) | async-done | bytes 196640 | tf_op jit(solution)/shard_map/all_to_all | solution.py:45
  234.4 5.3 %collective-permute-done.9.refs_4_ = f32[128,384]{1,0:T(8,128)S(1)} collective-permute-done((f32[128,384]{1,0:T(8,128)}, f32[128,384]{1,0:T(8,128)S(1)}, u32[]{:S(2)}, u32[]{:S(2)}) %collective-permute-start.9) | collective-permute-done | bytes 196640 | tf_op jit(solution)/shard_map/ppermute | solution.py:51
  249.9 6.1 %collective-permute-done.11.refs_5_ = f32[64,384]{1,0:T(8,128)S(1)} collective-permute-done((f32[64,384]{1,0:T(8,128)}, f32[64,384]{1,0:T(8,128)S(1)}, u32[]{:S(2)}, u32[]{:S(2)}) %collective-permute-start.11) | collective-permute-done | bytes 98336 | tf_op jit(solution)/shard_map/ppermute | solution.py:51
  255.9 8.7 %collective-permute-done.12.refs_11_ = f32[64,384]{1,0:T(8,128)S(1)} collective-permute-done((f32[64,384]{1,0:T(8,128)}, f32[64,384]{1,0:T(8,128)S(1)}, u32[]{:S(2)}, u32[]{:S(2)}) %collective-permute-start.12) | collective-permute-done | bytes 98336 | tf_op jit(solution)/shard_map/ppermute | solution.py:51
  268.0 12.1 %all-gather.5.cloned.1.call-done = bf16[896,768]{1,0:T(8,128)(2,1)} async-done(((bf16[224,768]{1,0:T(8,128)(2,1)}), bf16[896,768]{1,0:T(8,128)(2,1)}) %all-gather.5.cloned.1.call-update) | async-done | bytes 1376272 | tf_op jit(solution)/shard_map/all_gather | solution.py:614
  302.6 6.9 %collective-permute-done.17.refs_1_ = bf16[256,384]{1,0:T(8,128)(2,1)S(1)} collective-permute-done((bf16[256,384]{1,0:T(8,128)(2,1)}, bf16[256,384]{1,0:T(8,128)(2,1)S(1)}, u32[]{:S(2)}, u32[]{:S(2)}) %collective-permute-start.17) | collective-permute-done | bytes 196640 | tf_op jit(solution)/shard_map/ppermute | solution.py:51
  316.2 16.5 %collective-permute-done.19.refs_1_ = bf16[512,384]{1,0:T(8,128)(2,1)S(1)} collective-permute-done((bf16[512,384]{1,0:T(8,128)(2,1)}, bf16[512,384]{1,0:T(8,128)(2,1)S(1)}, u32[]{:S(2)}, u32[]{:S(2)}) %collective-permute-start.19) | collective-permute-done | bytes 393248 | tf_op jit(solution)/shard_map/ppermute | solution.py:51
  339.7 5.1 %fusion.26 = bf16[1024,768]{1,0:T(8,128)(2,1)} fusion(f32[1024,768]{1,0:T(8,128)} %shard_map.238, bf16[4,256,768]{2,1,0:T(8,128)(2,1)S(1)} %copy-done.4, f32[1024,768]{1,0:T(8,128)} %get-tuple-element.57, f32[768]{0:T(1024)S(1)} %get-tuple-element.114, f32[768]{0:T(1024)S(1)} %get-tuple-element.95, f32[768]{0:T(1024)S(1)} %get-tuple-element.113, ...), kind=kLoop, calls=%fused_computation.31 | loop fusion | flops 7864320 | bytes 9452544 | tf_op jit(solution)/shard_map/convert_element_type | solution.py:708
  346.0 5.1 %shard_map.248 = (f32[2304,384]{1,0:T(8,128)}, f32[384,768]{1,0:T(8,128)}, f32[1024,384]{1,0:T(8,128)}) custom-call(s32[1]{0:T(128)} %bitcast.33.core_ref, bf16[2048,384]{1,0:T(8,128)(2,1)} %shard_map.247.mine_ref, bf16[2048,384]{1,0:T(8,128)(2,1)} %copy-done.21), custom_call_target="tpu_custom_call" | custom-call | tf_op jit(solution)/shard_map/pallas_call | solution.py:529
  357.2 3.8 %shard_map.250 = f32[1643,768]{1,0:T(8,128)} custom-call(bf16[8,896,768]{2,1,0:T(8,128)(2,1)} %bitcast.137), custom_call_target="tpu_custom_call" | custom-call | tf_op jit(solution)/shard_map/pallas_call | solution.py:483
  361.0 10.0 %shard_map.249 = f32[5313,768]{1,0:T(8,128)} custom-call(bf16[8,896,768]{2,1,0:T(8,128)(2,1)} %bitcast.138), custom_call_target="tpu_custom_call" | custom-call | tf_op jit(solution)/shard_map/pallas_call | solution.py:483
  (213 shorter events, 140.1 us)
Async XLA Ops:
  10.0 16.6 %all-to-all-start = ((f32[32,1,1536]{2,1,0:T(1,128)}), f32[32,1,1536]{2,1,0:T(1,128)S(1)}, u32[]{:S(2)}, u32[]{:S(2)}) async-start(f32[32,1,1536]{2,1,0:T(1,128)} %broadcast_in_dim.21), calls=%async_computation | async-start | bytes 393216 | tf_op jit(solution)/shard_map/all_to_all | solution.py:45
  17.4 11.9 %collective-permute-start.1 = (bf16[4,11,768]{2,1,0:T(8,128)(2,1)S(1)}, bf16[4,11,768]{2,1,0:T(8,128)(2,1)S(1)}, u32[]{:S(2)}, u32[]{:S(2)}) collective-permute-start(bf16[4,11,768]{2,1,0:T(8,128)(2,1)S(1)} %get-tuple-element.103), channel_id=1, source_target_pairs={{4,0},{8,4},{12,8},{16,12},{20,16},{24,20},{28,24},{5,1},{9,5},{13... | collective-permute-start | bytes 202760 | tf_op jit(solution)/shard_map/ppermute | solution.py:236
  18.7 10.6 %collective-permute-start = (bf16[4,11,768]{2,1,0:T(8,128)(2,1)S(1)}, bf16[4,11,768]{2,1,0:T(8,128)(2,1)S(1)}, u32[]{:S(2)}, u32[]{:S(2)}) collective-permute-start(bf16[4,11,768]{2,1,0:T(8,128)(2,1)S(1)} %get-tuple-element.104), channel_id=1, source_target_pairs={{0,4},{4,8},{8,12},{12,16},{16,20},{20,24},{24,28},{1,5},{5,9},{9,... | collective-permute-start | bytes 202760 | tf_op jit(solution)/shard_map/ppermute | solution.py:235
  34.8 10.9 %all-to-all-start.1 = ((f32[32,1,768]{2,1,0:T(1,128)}), f32[32,1,768]{2,1,0:T(1,128)S(1)}, u32[]{:S(2)}, u32[]{:S(2)}) async-start(f32[32,1,768]{2,1,0:T(1,128)} %broadcast_in_dim.23), calls=%async_computation.1 | async-start | bytes 196608 | tf_op jit(solution)/shard_map/all_to_all | solution.py:45
  37.8 148.4 %reduce-scatter.3.cloned.1.call-start = ((), (), s32[]{:S(2)}) async-start(), calls=%async_computation.6 | async-start | bytes 12386304 | tf_op jit(solution)/shard_map/reduce_scatter | solution.py:613
  134.4 13.8 %all-to-all-start.2 = ((f32[32,1,768]{2,1,0:T(1,128)}), f32[32,1,768]{2,1,0:T(1,128)S(1)}, u32[]{:S(2)}, u32[]{:S(2)}) async-start(f32[32,1,768]{2,1,0:T(1,128)} %broadcast_in_dim.27), calls=%async_computation.3 | async-start | bytes 196608 | tf_op jit(solution)/shard_map/all_to_all | solution.py:45
  140.3 105.9 %reduce-scatter.5.cloned.1.call-start = ((), (), s32[]{:S(2)}) async-start(), calls=%async_computation.7 | async-start | bytes 1720320 | tf_op jit(solution)/shard_map/reduce_scatter | solution.py:613
  159.7 10.0 %collective-permute-start.3 = (f32[2048,384]{1,0:T(8,128)}, f32[2048,384]{1,0:T(8,128)S(1)}, u32[]{:S(2)}, u32[]{:S(2)}) collective-permute-start(f32[2048,384]{1,0:T(8,128)} %get-tuple-element.99), channel_id=1, source_target_pairs={{0,4},{4,0},{1,5},{5,1},{2,6},{6,2},{3,7},{7,3},{8,12},{12,8},{9,1... | collective-permute-start | bytes 9437192 | tf_op jit(solution)/shard_map/ppermute | solution.py:51
  161.1 14.0 %collective-permute-start.2 = (bf16[4,11,384]{2,1,0:T(8,128)(2,1)S(1)}, bf16[4,11,384]{2,1,0:T(8,128)(2,1)S(1)}, u32[]{:S(2)}, u32[]{:S(2)}) collective-permute-start(bf16[4,11,384]{2,1,0:T(8,128)(2,1)S(1)} %get-tuple-element.107), channel_id=1, source_target_pairs={{4,0},{8,4},{12,8},{16,12},{20,16},{24,20},{28,24},{5,1},{9,5},{13... | collective-permute-start | bytes 101384 | tf_op jit(solution)/shard_map/ppermute | solution.py:236
  162.4 12.7 %collective-permute-start.4 = (bf16[4,11,384]{2,1,0:T(8,128)(2,1)S(1)}, bf16[4,11,384]{2,1,0:T(8,128)(2,1)S(1)}, u32[]{:S(2)}, u32[]{:S(2)}) collective-permute-start(bf16[4,11,384]{2,1,0:T(8,128)(2,1)S(1)} %get-tuple-element.108), channel_id=1, source_target_pairs={{0,4},{4,8},{8,12},{12,16},{16,20},{20,24},{24,28},{1,5},{5,9},{9,... | collective-permute-start | bytes 101384 | tf_op jit(solution)/shard_map/ppermute | solution.py:235
  186.2 19.6 %collective-permute-start.5 = (f32[512,384]{1,0:T(8,128)}, f32[512,384]{1,0:T(8,128)S(1)}, u32[]{:S(2)}, u32[]{:S(2)}) collective-permute-start(f32[512,384]{1,0:T(8,128)} %get-tuple-element.58), channel_id=1, source_target_pairs={{0,8},{8,0},{1,9},{9,1},{2,10},{10,2},{3,11},{11,3},{4,12},{12,4},... | collective-permute-start | bytes 2359304 | tf_op jit(solution)/shard_map/ppermute | solution.py:51
  187.2 19.2 %collective-permute-start.6 = (f32[512,384]{1,0:T(8,128)}, f32[512,384]{1,0:T(8,128)S(1)}, u32[]{:S(2)}, u32[]{:S(2)}) collective-permute-start(f32[512,384]{1,0:T(8,128)} %get-tuple-element.59), channel_id=1, source_target_pairs={{0,16},{16,0},{1,17},{17,1},{2,18},{18,2},{3,19},{19,3},{4,20},{20... | collective-permute-start | bytes 2359304 | tf_op jit(solution)/shard_map/ppermute | solution.py:51
  210.7 16.6 %collective-permute-start.7 = (f32[256,384]{1,0:T(8,128)}, f32[256,384]{1,0:T(8,128)S(1)}, u32[]{:S(2)}, u32[]{:S(2)}) collective-permute-start(f32[256,384]{1,0:T(8,128)} %get-tuple-element.60), channel_id=1, source_target_pairs={{0,16},{16,0},{1,17},{17,1},{2,18},{18,2},{3,19},{19,3},{4,20},{20... | collective-permute-start | bytes 1179656 | tf_op jit(solution)/shard_map/ppermute | solution.py:51
  211.7 15.6 %collective-permute-start.8 = (f32[256,384]{1,0:T(8,128)}, f32[256,384]{1,0:T(8,128)S(1)}, u32[]{:S(2)}, u32[]{:S(2)}) collective-permute-start(f32[256,384]{1,0:T(8,128)} %get-tuple-element.61), channel_id=1, source_target_pairs={{0,8},{8,0},{1,9},{9,1},{2,10},{10,2},{3,11},{11,3},{4,12},{12,4},... | collective-permute-start | bytes 1179656 | tf_op jit(solution)/shard_map/ppermute | solution.py:51
  213.3 13.9 %all-to-all-start.3 = ((f32[32,1,1536]{2,1,0:T(1,128)}), f32[32,1,1536]{2,1,0:T(1,128)S(1)}, u32[]{:S(2)}, u32[]{:S(2)}) async-start(f32[32,1,1536]{2,1,0:T(1,128)} %broadcast_in_dim.28), calls=%async_computation.4 | async-start | bytes 393216 | tf_op jit(solution)/shard_map/all_to_all | solution.py:45
  217.9 62.1 %all-gather.5.cloned.1.call-start = ((), (), s32[]{:S(2)}) async-start(), calls=%async_computation.8 | async-start | bytes 1720320 | tf_op jit(solution)/shard_map/all_gather | solution.py:614
  231.7 11.2 %collective-permute-start.10 = (f32[128,384]{1,0:T(8,128)}, f32[128,384]{1,0:T(8,128)S(1)}, u32[]{:S(2)}, u32[]{:S(2)}) collective-permute-start(f32[128,384]{1,0:T(8,128)} %get-tuple-element.66), channel_id=1, source_target_pairs={{0,1},{1,0},{2,3},{3,2},{4,5},{5,4},{6,7},{7,6},{8,9},{9,8},{10,11... | collective-permute-start | bytes 589832 | tf_op jit(solution)/shard_map/ppermute | solution.py:51
  246.2 111.0 %all-gather.7.cloned.1.call-start = ((), (), s32[]{:S(2)}) async-start(), calls=%async_computation.9 | async-start | bytes 12386304 | tf_op jit(solution)/shard_map/all_gather | solution.py:614
  246.2 9.7 %collective-permute-start.11 = (f32[64,384]{1,0:T(8,128)}, f32[64,384]{1,0:T(8,128)S(1)}, u32[]{:S(2)}, u32[]{:S(2)}) collective-permute-start(f32[64,384]{1,0:T(8,128)} %get-tuple-element.70), channel_id=1, source_target_pairs={{0,2},{1,3},{2,0},{3,1},{4,6},{5,7},{6,4},{7,5},{8,10},{9,11},{10,... | collective-permute-start | bytes 294920 | tf_op jit(solution)/shard_map/ppermute | solution.py:51
  247.1 17.6 %collective-permute-start.12 = (f32[64,384]{1,0:T(8,128)}, f32[64,384]{1,0:T(8,128)S(1)}, u32[]{:S(2)}, u32[]{:S(2)}) collective-permute-start(f32[64,384]{1,0:T(8,128)} %get-tuple-element.71), channel_id=1, source_target_pairs={{0,2},{1,3},{2,0},{3,1},{4,6},{5,7},{6,4},{7,5},{8,10},{9,11},{10,... | collective-permute-start | bytes 294920 | tf_op jit(solution)/shard_map/ppermute | solution.py:51
  299.0 10.5 %collective-permute-start.17 = (bf16[256,384]{1,0:T(8,128)(2,1)}, bf16[256,384]{1,0:T(8,128)(2,1)S(1)}, u32[]{:S(2)}, u32[]{:S(2)}) collective-permute-start(bf16[256,384]{1,0:T(8,128)(2,1)} %get-tuple-element.79.refs_0_), channel_id=1, source_target_pairs={{0,16},{16,0},{1,17},{17,1},{2,18},{18,2},{3,19},{19,3},{4,20},{20... | collective-permute-start | bytes 589832 | tf_op jit(solution)/shard_map/ppermute | solution.py:51
  300.8 8.7 %collective-permute-start.18 = (bf16[256,384]{1,0:T(8,128)(2,1)}, bf16[256,384]{1,0:T(8,128)(2,1)S(1)}, u32[]{:S(2)}, u32[]{:S(2)}) collective-permute-start(bf16[256,384]{1,0:T(8,128)(2,1)} %get-tuple-element.80.refs_2_), channel_id=1, source_target_pairs={{0,8},{8,0},{1,9},{9,1},{2,10},{10,2},{3,11},{11,3},{4,12},{12,4},... | collective-permute-start | bytes 589832 | tf_op jit(solution)/shard_map/ppermute | solution.py:51
  313.6 19.1 %collective-permute-start.19 = (bf16[512,384]{1,0:T(8,128)(2,1)}, bf16[512,384]{1,0:T(8,128)(2,1)S(1)}, u32[]{:S(2)}, u32[]{:S(2)}) collective-permute-start(bf16[512,384]{1,0:T(8,128)(2,1)} %get-tuple-element.81.refs_0_), channel_id=1, source_target_pairs={{0,8},{8,0},{1,9},{9,1},{2,10},{10,2},{3,11},{11,3},{4,12},{12,4},... | collective-permute-start | bytes 1179656 | tf_op jit(solution)/shard_map/ppermute | solution.py:51
  315.1 19.9 %collective-permute-start.20 = (bf16[512,384]{1,0:T(8,128)(2,1)}, bf16[512,384]{1,0:T(8,128)(2,1)S(1)}, u32[]{:S(2)}, u32[]{:S(2)}) collective-permute-start(bf16[512,384]{1,0:T(8,128)(2,1)} %get-tuple-element.82.refs_2_), channel_id=1, source_target_pairs={{0,16},{16,0},{1,17},{17,1},{2,18},{18,2},{3,19},{19,3},{4,20},{20... | collective-permute-start | bytes 1179656 | tf_op jit(solution)/shard_map/ppermute | solution.py:51
  (51 other events, 265.6 us)
Sparse Core Ops, SparseCore 0:
  101.7 84.4 reduce-scatter.2
  188.5 31.8 reduce-scatter.4
  246.3 33.6 all-gather.4
  281.9 75.2 all-gather.6

commit v3 on v2

--- a/solution.py
+++ b/solution.py
@@ -621,7 +621,6 @@
     output_grad = head_back(humans, windows, mouse, human, slopes)
     to_core = lambda value: swap(value, CORE)
     chips = lax.axis_size(CHIPS)
-    unit = 16 * chips
 
     def after_head(output_grad):
         branch_grad = output_grad.astype(BF16)
@@ -656,14 +655,15 @@
             bias_grads[0, :tracks_mouse],
         ]
     )
-    weight_rows = pl.cdiv(4 * width * middle + sums.size, middle)
-    all_rows = pl.cdiv(weight_rows, 4 * unit) * 4 * unit
+    vector_rows = pl.cdiv(sums.size, middle)
+    grain = 32 * chips
+    all_rows = pl.cdiv(4 * width + vector_rows, grain) * grain
     half = all_rows // 2
 
     def conv_work(dilated_grad, proj_grad, sums):
         parts = [rows_product(rows, dilated_grad) for rows in shifted] + [proj_grad]
-        fill = (all_rows - 4 * width) * middle - sums.size
-        parts.append(jnp.pad(sums, (0, fill)).reshape(-1, middle))
+        rows = jnp.pad(sums, (0, vector_rows * middle - sums.size)).reshape(-1, middle)
+        parts.append(jnp.pad(rows, ((0, all_rows - 4 * width - vector_rows), (0, 0))))
         grads = jnp.concatenate(parts, axis=0)
         return lax.dynamic_slice_in_dim(grads, (1 - core[0]) * half, half, 0), grads
 
@@ -692,10 +692,9 @@
     everyone = to_all(sent)
     summed, in_grad = tie(summed, in_grad)
     summed = scatter(summed, "batch")
-    weights.step()
-    everyone = weights.step(everyone)
     summed = weights.step(summed)
     summed = gather(summed, "batch").reshape(-1, width)
+    everyone = weights.step(everyone)
     summed = weights.step(summed)
     summed = gather(summed, BINS)
 
@@ -708,20 +707,28 @@
         return input_grad.astype(BF16), shift_in_grad, gain_in_grad
 
     input_grad, shift_in_grad, gain_in_grad = last_work(everyone, output_grad, in_grad)
+    while weights.level < 2 * weights.levels - 1:
+        weights.step()
+    input_grad = weights.step(input_grad)
     while not weights.done():
         weights.step()
     weights_mine = weights.shares[0]
+    weights_other = to_core(weights_mine)
+    summed = summed.reshape(lax.axis_size(BINS), -1, width)
+    head_mouse_grad = widen_head(tracks_mouse, summed, 0)
+    head_human_grad = widen_head(tracks_human, summed, mouse_tiles * TILE)
+    weights_other, head_mouse_grad, head_human_grad = tie(
+        weights_other, head_mouse_grad, head_human_grad
+    )
     conv_total, proj_total, sums_total = finish_weights(
-        core, weights_mine, to_core(weights_mine), 3 * width, (middle, width)
+        core, weights_mine, weights_other, 3 * width, (middle, width)
     )
     conv_total = conv_total.reshape(3, width, middle)
-    sums_total = sums_total.reshape(-1)
+    sums_total = sums_total[:vector_rows].reshape(-1)
     ends = [0, width, width + tracks_human, width + tracks_human + tracks_mouse]
     proj_bias_total, bias_human_grad, bias_mouse_grad = [
         sums_total[low:high] for low, high in zip(ends[:-1], ends[1:])
     ]
-    head_mouse_grad = widen_head(tracks_mouse, summed, 0)
-    head_human_grad = widen_head(tracks_human, summed, mouse_tiles * TILE)
     return (
         block_out.reshape(windows, span, width),
         input_grad.reshape(windows, span, width),

time: 385 us -> 374 us (0.971)
  local copies, waits for them, and re-layouts: 36.4 us -> 27.7 us
  Pallas kernels: 115 us -> 110 us
    reduce_scatter x2, waiting for transfers between devices: 3.43 us -> 18.6 us  [on_device(): lax.psum_scatter(value, axes, scatter_dimension=0, tiled=True)]
    ppermute x18, waiting for transfers between devices: 73.5 us -> 65.9 us  [swap(): return lax.ppermute(value, axis, [(i, i ^ mask) for i in range(size)])]
    pallas_call x5 -> x3, Pallas kernels: 15.2 us -> 9.54 us  [sum_parts(): pl.pallas_call(functools.partial(sum_body, counts=counts), grid_spec=pltp...]
    all_to_all x4, starting transfers between devices: 20.6 us -> 15.9 us  [to_all(): return lax.all_to_all(sent, axes, 0, 0, tiled=True)]
    reshape x2, local copies, waits for them, and re-layouts: 4.28 us -> 0.02 us  [the longest x1 0.01 us: conv_work(): jnp.pad(sums, (0, vector_rows * middle - sums.size)).reshape(-1, middle)]
    all_gather x2, waiting for transfers between devices: 14.1 us -> 10.1 us  [on_device(): gather = lambda value, axes: lax.all_gather(value, axes)]
    unnamed x92 -> x94, local copies, waits for them, and re-layouts: 14.5 us -> 11.9 us
    pallas_call x4 -> x3, Pallas kernels: 10.9 us -> 8.32 us  [join_parts(): pl.pallas_call(functools.partial(join_body, count=len(parts), stacked=sta...]
  transfers between devices with their start and end apart: 30 -> 30, of which waited for: 20 -> 22; matrix products, arithmetic and copies ran while one was open for 15% -> 14% of each run, Pallas kernels for 14% -> 15%
where the time goes in v3:
time: 374 us; the launch traced here: 367 us
  waiting for transfers between devices  114 us (30%)
  Pallas kernels  110 us (29%)
  starting transfers between devices  46.1 us (12%)
  local copies, waits for them, and re-layouts  27.7 us (7%)
  matrix products  27.6 us (7%)
  other arithmetic  26.4 us (7%)
  between operations  14.8 us (4%)
    ppermute x18, waiting for transfers between devices, swap(): return lax.ppermute(value, axis, [(i, i ^ mask) for i in range(size)])  65.9 us
    pallas_call x1, Pallas kernels, head(): pl.pallas_call(functools.partial(head_body, mouse_tiles=mouse_tiles, trac...  51.1 us
    pallas_call x1, Pallas kernels, head_back(): pl.pallas_call(functools.partial(back_body, mouse_tiles=mouse_tiles, trac...  22.7 us
    ppermute x18, starting transfers between devices, swap(): return lax.ppermute(value, axis, [(i, i ^ mask) for i in range(size)])  21.4 us
    all_to_all x4, waiting for transfers between devices, to_all(): return lax.all_to_all(sent, axes, 0, 0, tiled=True)  19.2 us
    reduce_scatter x2, waiting for transfers between devices, on_device(): lax.psum_scatter(value, axes, scatter_dimension=0, tiled=True)  18.6 us
    all_to_all x4, starting transfers between devices, to_all(): return lax.all_to_all(sent, axes, 0, 0, tiled=True)  15.9 us
    pallas_call x2, Pallas kernels, widen_head(): pl.pallas_call(widen_body, grid=(pl.cdiv(tracks, block),), in_specs=[pl.B...  13.8 us
  transfers between devices with their start and end apart: 30, of which 22 were waited for; matrix products, arithmetic and copies ran while one was open for 14% of the time, Pallas kernels for 15%

profile of v3, /device:TPU:0, one launch (start us, length us, event | category | flops | bytes accessed | tf_op | source)
XLA Modules:
  0.0 366.6 jit_solution(13703870509808416657)
XLA Ops:
  10.0 7.3 %all-to-all-start = ((f32[32,1,1536]{2,1,0:T(1,128)}), f32[32,1,1536]{2,1,0:T(1,128)S(1)}, u32[]{:S(2)}, u32[]{:S(2)}) async-start(f32[32,1,1536]{2,1,0:T(1,128)} %broadcast_in_dim.21), calls=%async_computation | async-start | bytes 393216 | tf_op jit(solution)/shard_map/all_to_all | solution.py:45
  21.7 4.9 %all-to-all-done = f32[32,1,1536]{2,1,0:T(1,128)S(1)} async-done(((f32[32,1,1536]{2,1,0:T(1,128)}), f32[32,1,1536]{2,1,0:T(1,128)S(1)}, u32[]{:S(2)}, u32[]{:S(2)}) %all-to-all-start) | async-done | bytes 196640 | tf_op jit(solution)/shard_map/all_to_all | solution.py:45
  40.6 5.3 %all-to-all-done.1 = f32[32,1,768]{2,1,0:T(1,128)S(1)} async-done(((f32[32,1,768]{2,1,0:T(1,128)}), f32[32,1,768]{2,1,0:T(1,128)S(1)}, u32[]{:S(2)}, u32[]{:S(2)}) %all-to-all-start.1) | async-done | bytes 98336 | tf_op jit(solution)/shard_map/all_to_all | solution.py:45
  46.6 3.9 %fusion.12.rows_ref = bf16[1024,768]{1,0:T(8,128)(2,1)} fusion(bf16[4,256,768]{2,1,0:T(8,128)(2,1)S(1)} %copy-done.3, bf16[384,768]{1,0:T(8,128)(2,1)S(1)} %copy-done, f32[768]{0:T(1024)S(1)} %copy-done.43, f32[1024,384]{1,0:T(8,128)} %get-tuple-element.135, f32[384]{0:T(512)S(1)} %copy-done.44, f32[384]{0:T(512)S(1)} %copy-done.42, ...), kind=kOutput, calls=%fused_computation.17 | convolution fusion | flops 611057664 | bytes 5317632 | tf_op jit(solution)/shard_map/dot_general | solution.py:596
  53.2 51.1 %shard_map.237 = (bf16[7168,768]{1,0:T(8,128)(2,1)}, bf16[7168,1024]{1,0:T(8,128)(2,1)}, f32[1,7168]{1,0:T(1,128)}) custom-call(s32[4]{0:T(128)} %species_ref.1, s32[4]{0:T(128)} %get-tuple-element.54.windows_ref, s32[1]{0:T(128)} %bitcast.11.humans_ref, bf16[1643,768]{1,0:T(8,128)(2,1)} %bitcast.147, bf16[5313,768]{1,0:T(8,128)(2,1)} %bitcast.144, ...), custom_call_target="tpu_custom_call" | custom-call | flops 22548578304 | bytes 66060288 | tf_op jit(solution)/shard_map/pallas_call | solution.py:376
  106.6 22.7 %shard_map.238 = f32[1024,768]{1,0:T(8,128)} custom-call(s32[1]{0:T(128)} %bitcast.11.humans_ref, bf16[1643,768]{1,0:T(8,128)(2,1)} %bitcast.148, bf16[5313,768]{1,0:T(8,128)(2,1)} %bitcast.145, bf16[7168,1024]{1,0:T(8,128)(2,1)} %get-tuple-element.55.grads_ref), custom_call_target="tpu_custom_call" | custom-call | flops 11274289152 | bytes 25690112 | tf_op jit(solution)/shard_map/pallas_call | solution.py:449
  131.7 4.6 %fusion.53 = (f32[384]{0:T(512)S(1)}, f32[384]{0:T(512)S(1)}, f32[1024,384]{1,0:T(8,128)}) fusion(f32[384]{0:T(512)S(1)} %get-tuple-element.133, f32[1024,384]{1,0:T(8,128)S(1)} %copy-done.5, f32[384]{0:T(512)S(1)} %get-tuple-element.132, f32[384]{0:T(512)S(1)} %copy-done.44, f32[384]{0:T(512)S(1)} %copy-done.42, bf16[384,768]{1,0:T(8,128)(2,1)S(1)} %copy-done, ...), kind=kOutput, calls=%fused_computation.112 | convolution fusion | flops 611056896 | bytes 6890496 | tf_op jit(solution)/shard_map/dot_general | solution.py:210
  143.9 3.6 all-to-all-done.2
  163.5 3.7 %fusion.33 = f32[1024,768]{1,0:T(8,128)} fusion(bf16[1024,384]{1,0:T(8,128)(2,1)S(1)} %multiply_convert_fusion, bf16[3,768,384]{2,1,0:T(8,128)(2,1)} %param.17), kind=kOutput, calls=%fused_computation.58 | convolution fusion | flops 603979776 | bytes 4521984 | tf_op jit(solution)/shard_map/dot_general | solution.py:210
  168.8 3.5 shard_map.239
  175.5 4.3 %fusion.52 = (f32[768]{0:T(1024)S(1)}, f32[768]{0:T(1024)S(1)}, f32[1024,768]{1,0:T(8,128)}) fusion(f32[768]{0:T(1024)S(1)} %get-tuple-element.129, f32[768]{0:T(1024)S(1)} %get-tuple-element.128, bf16[4,256,768]{2,1,0:T(8,128)(2,1)S(1)} %copy-done.4, f32[768]{0:T(1024)S(1)} %copy-done.30, f32[768]{0:T(1024)S(1)} %copy-done.29, ...), kind=kOutput, calls=%fused_computation.111 | convolution fusion | flops 618920448 | bytes 12408832 | tf_op jit(solution)/shard_map/dot_general | solution.py:210
  179.8 6.6 %reduce-scatter.3.cloned.1.call-done = bf16[896,768]{1,0:T(8,128)(2,1)} async-done(((bf16[7168,768]{1,0:T(8,128)(2,1)}), bf16[896,768]{1,0:T(8,128)(2,1)}) %reduce-scatter.3.cloned.1.call-update) | async-done | bytes 1376272 | tf_op jit(solution)/shard_map/reduce_scatter | solution.py:613
  189.1 14.8 %collective-permute-done.4.refs_2_ = f32[448,384]{1,0:T(8,128)S(1)} collective-permute-done((f32[448,384]{1,0:T(8,128)}, f32[448,384]{1,0:T(8,128)S(1)}, u32[]{:S(2)}, u32[]{:S(2)}) %collective-permute-start.4) | collective-permute-done | bytes 688160 | tf_op jit(solution)/shard_map/ppermute | solution.py:51
  208.9 12.0 %reduce-scatter.5.cloned.1.call-done = bf16[224,768]{1,0:T(8,128)(2,1)} async-done(((bf16[896,768]{1,0:T(8,128)(2,1)}), bf16[224,768]{1,0:T(8,128)(2,1)}) %reduce-scatter.5.cloned.1.call-update) | async-done | bytes 344080 | tf_op jit(solution)/shard_map/reduce_scatter | solution.py:613
  229.2 5.4 %all-to-all-done.3 = f32[32,1,1536]{2,1,0:T(1,128)S(1)} async-done(((f32[32,1,1536]{2,1,0:T(1,128)}), f32[32,1,1536]{2,1,0:T(1,128)S(1)}, u32[]{:S(2)}, u32[]{:S(2)}) %all-to-all-start.3) | async-done | bytes 196640 | tf_op jit(solution)/shard_map/all_to_all | solution.py:45
  244.2 14.0 %collective-permute-done.9 = f32[112,384]{1,0:T(8,128)S(1)} collective-permute-done((f32[112,384]{1,0:T(8,128)}, f32[112,384]{1,0:T(8,128)S(1)}, u32[]{:S(2)}, u32[]{:S(2)}) %collective-permute-start.9) | collective-permute-done | bytes 172064 | tf_op jit(solution)/shard_map/ppermute | solution.py:51
  258.1 3.8 %collective-permute-done.10 = f32[112,384]{1,0:T(8,128)S(1)} collective-permute-done((f32[112,384]{1,0:T(8,128)}, f32[112,384]{1,0:T(8,128)S(1)}, u32[]{:S(2)}, u32[]{:S(2)}) %collective-permute-start.10) | collective-permute-done | bytes 172064 | tf_op jit(solution)/shard_map/ppermute | solution.py:51
  267.0 5.0 %collective-permute-done.11 = f32[56,384]{1,0:T(8,128)S(1)} collective-permute-done((f32[56,384]{1,0:T(8,128)S(1)}, f32[56,384]{1,0:T(8,128)S(1)}, u32[]{:S(2)}, u32[]{:S(2)}) %collective-permute-start.11) | collective-permute-done | bytes 86048 | tf_op jit(solution)/shard_map/ppermute | solution.py:51
  294.0 6.3 %fusion.26 = bf16[1024,768]{1,0:T(8,128)(2,1)} fusion(f32[1024,768]{1,0:T(8,128)} %shard_map.238, bf16[4,256,768]{2,1,0:T(8,128)(2,1)S(1)} %copy-done.4, f32[1024,768]{1,0:T(8,128)} %get-tuple-element.83, f32[768]{0:T(1024)S(1)} %get-tuple-element.130, f32[768]{0:T(1024)S(1)} %get-tuple-element.103, f32[768]{0:T(1024)S(1)} %copy-done.34, ...), kind=kLoop, calls=%fused_computation.31 | loop fusion | flops 7864320 | bytes 9452544 | tf_op jit(solution)/shard_map/convert_element_type | solution.py:707
  307.2 14.1 %collective-permute-done.19.refs_1_ = bf16[448,384]{1,0:T(8,128)(2,1)S(1)} collective-permute-done((bf16[448,384]{1,0:T(8,128)(2,1)}, bf16[448,384]{1,0:T(8,128)(2,1)S(1)}, u32[]{:S(2)}, u32[]{:S(2)}) %collective-permute-start.19) | collective-permute-done | bytes 344096 | tf_op jit(solution)/shard_map/ppermute | solution.py:51
  326.6 10.1 %all-gather.7.cloned.1.call-done = bf16[7168,768]{1,0:T(8,128)(2,1)} async-done(((bf16[896,768]{1,0:T(8,128)(2,1)}), bf16[7168,768]{1,0:T(8,128)(2,1)}) %all-gather.7.cloned.1.call-update) | async-done | bytes 11010064 | tf_op jit(solution)/shard_map/all_gather | solution.py:614
  336.7 3.8 %shard_map.245 = f32[1643,768]{1,0:T(8,128)} custom-call(bf16[8,896,768]{2,1,0:T(8,128)(2,1)} %bitcast.124), custom_call_target="tpu_custom_call" | custom-call | tf_op jit(solution)/shard_map/pallas_call | solution.py:483
  340.6 10.0 %shard_map.246 = f32[5313,768]{1,0:T(8,128)} custom-call(bf16[8,896,768]{2,1,0:T(8,128)(2,1)} %bitcast.125), custom_call_target="tpu_custom_call" | custom-call | tf_op jit(solution)/shard_map/pallas_call | solution.py:483
  351.7 4.5 %shard_map.247 = (f32[2304,384]{1,0:T(8,128)}, f32[384,768]{1,0:T(8,128)}, f32[512,384]{1,0:T(8,128)}) custom-call(s32[1]{0:T(128)} %bitcast.36.core_ref, bf16[1792,384]{1,0:T(8,128)(2,1)} %shard_map.244.mine_ref, bf16[1792,384]{1,0:T(8,128)(2,1)} %copy-done.18), custom_call_target="tpu_custom_call" | custom-call | tf_op jit(solution)/shard_map/pallas_call | solution.py:529
  (215 shorter events, 126.2 us)
Async XLA Ops:
  10.0 16.6 %all-to-all-start = ((f32[32,1,1536]{2,1,0:T(1,128)}), f32[32,1,1536]{2,1,0:T(1,128)S(1)}, u32[]{:S(2)}, u32[]{:S(2)}) async-start(f32[32,1,1536]{2,1,0:T(1,128)} %broadcast_in_dim.21), calls=%async_computation | async-start | bytes 393216 | tf_op jit(solution)/shard_map/all_to_all | solution.py:45
  17.4 12.5 %collective-permute-start.1 = (bf16[4,11,768]{2,1,0:T(8,128)(2,1)S(1)}, bf16[4,11,768]{2,1,0:T(8,128)(2,1)S(1)}, u32[]{:S(2)}, u32[]{:S(2)}) collective-permute-start(bf16[4,11,768]{2,1,0:T(8,128)(2,1)S(1)} %get-tuple-element.115), channel_id=1, source_target_pairs={{4,0},{8,4},{12,8},{16,12},{20,16},{24,20},{28,24},{5,1},{9,5},{13... | collective-permute-start | bytes 202760 | tf_op jit(solution)/shard_map/ppermute | solution.py:236
  18.7 11.2 %collective-permute-start = (bf16[4,11,768]{2,1,0:T(8,128)(2,1)S(1)}, bf16[4,11,768]{2,1,0:T(8,128)(2,1)S(1)}, u32[]{:S(2)}, u32[]{:S(2)}) collective-permute-start(bf16[4,11,768]{2,1,0:T(8,128)(2,1)S(1)} %get-tuple-element.116), channel_id=1, source_target_pairs={{0,4},{4,8},{8,12},{12,16},{16,20},{20,24},{24,28},{1,5},{5,9},{9,... | collective-permute-start | bytes 202760 | tf_op jit(solution)/shard_map/ppermute | solution.py:235
  35.3 10.5 %all-to-all-start.1 = ((f32[32,1,768]{2,1,0:T(1,128)}), f32[32,1,768]{2,1,0:T(1,128)S(1)}, u32[]{:S(2)}, u32[]{:S(2)}) async-start(f32[32,1,768]{2,1,0:T(1,128)} %broadcast_in_dim.23), calls=%async_computation.1 | async-start | bytes 196608 | tf_op jit(solution)/shard_map/all_to_all | solution.py:45
  37.9 148.5 %reduce-scatter.3.cloned.1.call-start = ((), (), s32[]{:S(2)}) async-start(), calls=%async_computation.6 | async-start | bytes 12386304 | tf_op jit(solution)/shard_map/reduce_scatter | solution.py:613
  137.0 10.5 %all-to-all-start.2 = ((f32[32,1,768]{2,1,0:T(1,128)}), f32[32,1,768]{2,1,0:T(1,128)S(1)}, u32[]{:S(2)}, u32[]{:S(2)}) async-start(f32[32,1,768]{2,1,0:T(1,128)} %broadcast_in_dim.27), calls=%async_computation.2 | async-start | bytes 196608 | tf_op jit(solution)/shard_map/all_to_all | solution.py:45
  139.6 81.3 %reduce-scatter.5.cloned.1.call-start = ((), (), s32[]{:S(2)}) async-start(), calls=%async_computation.7 | async-start | bytes 1720320 | tf_op jit(solution)/shard_map/reduce_scatter | solution.py:613
  158.5 8.8 %collective-permute-start.2 = (f32[1792,384]{1,0:T(8,128)}, f32[1792,384]{1,0:T(8,128)S(1)}, u32[]{:S(2)}, u32[]{:S(2)}) collective-permute-start(f32[1792,384]{1,0:T(8,128)} %get-tuple-element.111), channel_id=1, source_target_pairs={{0,4},{4,0},{1,5},{5,1},{2,6},{6,2},{3,7},{7,3},{8,12},{12,8},{9,1... | collective-permute-start | bytes 8257544 | tf_op jit(solution)/shard_map/ppermute | solution.py:51
  159.2 13.2 %collective-permute-start.6 = (bf16[4,11,384]{2,1,0:T(8,128)(2,1)S(1)}, bf16[4,11,384]{2,1,0:T(8,128)(2,1)S(1)}, u32[]{:S(2)}, u32[]{:S(2)}) collective-permute-start(bf16[4,11,384]{2,1,0:T(8,128)(2,1)S(1)} %get-tuple-element.119), channel_id=1, source_target_pairs={{4,0},{8,4},{12,8},{16,12},{20,16},{24,20},{28,24},{5,1},{9,5},{13... | collective-permute-start | bytes 101384 | tf_op jit(solution)/shard_map/ppermute | solution.py:236
  160.5 11.9 %collective-permute-start.3 = (bf16[4,11,384]{2,1,0:T(8,128)(2,1)S(1)}, bf16[4,11,384]{2,1,0:T(8,128)(2,1)S(1)}, u32[]{:S(2)}, u32[]{:S(2)}) collective-permute-start(bf16[4,11,384]{2,1,0:T(8,128)(2,1)S(1)} %get-tuple-element.120), channel_id=1, source_target_pairs={{0,4},{4,8},{8,12},{12,16},{16,20},{20,24},{24,28},{1,5},{5,9},{9,... | collective-permute-start | bytes 101384 | tf_op jit(solution)/shard_map/ppermute | solution.py:235
  186.4 76.8 %all-gather.5.cloned.1.call-start = ((), (), s32[]{:S(2)}) async-start(), calls=%async_computation.8 | async-start | bytes 1720320 | tf_op jit(solution)/shard_map/all_gather | solution.py:614
  186.5 17.4 %collective-permute-start.4 = (f32[448,384]{1,0:T(8,128)}, f32[448,384]{1,0:T(8,128)S(1)}, u32[]{:S(2)}, u32[]{:S(2)}) collective-permute-start(f32[448,384]{1,0:T(8,128)} %get-tuple-element.59), channel_id=1, source_target_pairs={{0,8},{8,0},{1,9},{9,1},{2,10},{10,2},{3,11},{11,3},{4,12},{12,4},... | collective-permute-start | bytes 2064392 | tf_op jit(solution)/shard_map/ppermute | solution.py:51
  187.9 17.1 %collective-permute-start.5 = (f32[448,384]{1,0:T(8,128)}, f32[448,384]{1,0:T(8,128)S(1)}, u32[]{:S(2)}, u32[]{:S(2)}) collective-permute-start(f32[448,384]{1,0:T(8,128)} %get-tuple-element.60), channel_id=1, source_target_pairs={{0,16},{16,0},{1,17},{17,1},{2,18},{18,2},{3,19},{19,3},{4,20},{20... | collective-permute-start | bytes 2064392 | tf_op jit(solution)/shard_map/ppermute | solution.py:51
  221.8 12.8 %all-to-all-start.3 = ((f32[32,1,1536]{2,1,0:T(1,128)}), f32[32,1,1536]{2,1,0:T(1,128)S(1)}, u32[]{:S(2)}, u32[]{:S(2)}) async-start(f32[32,1,1536]{2,1,0:T(1,128)} %broadcast_in_dim.28), calls=%async_computation.5 | async-start | bytes 393216 | tf_op jit(solution)/shard_map/all_to_all | solution.py:45
  225.2 111.5 %all-gather.7.cloned.1.call-start = ((), (), s32[]{:S(2)}) async-start(), calls=%async_computation.9 | async-start | bytes 12386304 | tf_op jit(solution)/shard_map/all_gather | solution.py:614
  225.3 12.5 %collective-permute-start.7 = (f32[224,384]{1,0:T(8,128)}, f32[224,384]{1,0:T(8,128)S(1)}, u32[]{:S(2)}, u32[]{:S(2)}) collective-permute-start(f32[224,384]{1,0:T(8,128)} %get-tuple-element.66), channel_id=1, source_target_pairs={{0,16},{16,0},{1,17},{17,1},{2,18},{18,2},{3,19},{19,3},{4,20},{20... | collective-permute-start | bytes 1032200 | tf_op jit(solution)/shard_map/ppermute | solution.py:51
  227.1 11.2 %collective-permute-start.8 = (f32[224,384]{1,0:T(8,128)}, f32[224,384]{1,0:T(8,128)S(1)}, u32[]{:S(2)}, u32[]{:S(2)}) collective-permute-start(f32[224,384]{1,0:T(8,128)} %get-tuple-element.67), channel_id=1, source_target_pairs={{0,8},{8,0},{1,9},{9,1},{2,10},{10,2},{3,11},{11,3},{4,12},{12,4},... | collective-permute-start | bytes 1032200 | tf_op jit(solution)/shard_map/ppermute | solution.py:51
  242.1 16.0 %collective-permute-start.9 = (f32[112,384]{1,0:T(8,128)}, f32[112,384]{1,0:T(8,128)S(1)}, u32[]{:S(2)}, u32[]{:S(2)}) collective-permute-start(f32[112,384]{1,0:T(8,128)} %get-tuple-element.70), channel_id=1, source_target_pairs={{0,1},{1,0},{2,3},{3,2},{4,5},{5,4},{6,7},{7,6},{8,9},{9,8},{10,11... | collective-permute-start | bytes 516104 | tf_op jit(solution)/shard_map/ppermute | solution.py:51
  243.8 18.2 %collective-permute-start.10 = (f32[112,384]{1,0:T(8,128)}, f32[112,384]{1,0:T(8,128)S(1)}, u32[]{:S(2)}, u32[]{:S(2)}) collective-permute-start(f32[112,384]{1,0:T(8,128)} %get-tuple-element.71), channel_id=1, source_target_pairs={{0,1},{1,0},{2,3},{3,2},{4,5},{5,4},{6,7},{7,6},{8,9},{9,8},{10,11... | collective-permute-start | bytes 516104 | tf_op jit(solution)/shard_map/ppermute | solution.py:51
  264.2 9.4 %collective-permute-start.12 = (f32[56,384]{1,0:T(8,128)S(1)}, f32[56,384]{1,0:T(8,128)S(1)}, u32[]{:S(2)}, u32[]{:S(2)}) collective-permute-start(f32[56,384]{1,0:T(8,128)S(1)} %get-tuple-element.74), channel_id=1, source_target_pairs={{0,2},{1,3},{2,0},{3,1},{4,6},{5,7},{6,4},{7,5},{8,10},{9,11},{10,... | collective-permute-start | bytes 258056 | tf_op jit(solution)/shard_map/ppermute | solution.py:51
  291.1 9.3 %collective-permute-start.17 = (bf16[224,384]{1,0:T(8,128)(2,1)}, bf16[224,384]{1,0:T(8,128)(2,1)S(1)}, u32[]{:S(2)}, u32[]{:S(2)}) collective-permute-start(bf16[224,384]{1,0:T(8,128)(2,1)} %get-tuple-element.79.refs_0_), channel_id=1, source_target_pairs={{0,16},{16,0},{1,17},{17,1},{2,18},{18,2},{3,19},{19,3},{4,20},{20... | collective-permute-start | bytes 516104 | tf_op jit(solution)/shard_map/ppermute | solution.py:51
  304.4 16.9 %collective-permute-start.19 = (bf16[448,384]{1,0:T(8,128)(2,1)}, bf16[448,384]{1,0:T(8,128)(2,1)S(1)}, u32[]{:S(2)}, u32[]{:S(2)}) collective-permute-start(bf16[448,384]{1,0:T(8,128)(2,1)} %get-tuple-element.86.refs_0_), channel_id=1, source_target_pairs={{0,8},{8,0},{1,9},{9,1},{2,10},{10,2},{3,11},{11,3},{4,12},{12,4},... | collective-permute-start | bytes 1032200 | tf_op jit(solution)/shard_map/ppermute | solution.py:51
  306.6 16.1 %collective-permute-start.20 = (bf16[448,384]{1,0:T(8,128)(2,1)}, bf16[448,384]{1,0:T(8,128)(2,1)S(1)}, u32[]{:S(2)}, u32[]{:S(2)}) collective-permute-start(bf16[448,384]{1,0:T(8,128)(2,1)} %get-tuple-element.87.refs_2_), channel_id=1, source_target_pairs={{0,16},{16,0},{1,17},{17,1},{2,18},{18,2},{3,19},{19,3},{4,20},{20... | collective-permute-start | bytes 1032200 | tf_op jit(solution)/shard_map/ppermute | solution.py:51
  326.6 23.9 %collective-permute-start.21 = (bf16[1792,384]{1,0:T(8,128)(2,1)}, bf16[1792,384]{1,0:T(8,128)(2,1)S(1)}, u32[]{:S(2)}, u32[]{:S(2)}) collective-permute-start(bf16[1792,384]{1,0:T(8,128)(2,1)} %shard_map.244.mine_ref), channel_id=1, source_target_pairs={{0,4},{4,0},{1,5},{5,1},{2,6},{6,2},{3,7},{7,3},{8,12},{12,8},{9,1... | collective-permute-start | bytes 4128776 | tf_op jit(solution)/shard_map/ppermute | solution.py:51
  (52 other events, 509.8 us)
Sparse Core Ops, SparseCore 0:
  104.4 81.9 reduce-scatter.2
  188.7 32.2 reduce-scatter.4
  222.6 36.7 all-gather.4
  263.4 73.3 all-gather.6
